TPU v7x, 256 devices: a whole 4x4x8 slice. The times are simulated.
256 devices in a mesh: gx: 16 (over y, x), gy: 16 (over z, core).
Axes of the slice: x: 4, y: 4, z: 8, core: 2. Of those that a mesh axis runs over, the one named last changes fastest.
Arguments:
- drawdown: float32 [16, 2048, 2048], P(None, 'gx', 'gy'), may hold values from -6 to 6
- step_ratio: float32 [16, 2048, 2048], P(None, 'gx', 'gy'), may hold values from 3000 to 30000
- layer_class: int32 [16, 2048, 2048], P(None, 'gx', 'gy'), may hold values from 0 to 7
- class_conductance: float32 [8], replicated, may hold values from 3 to 30
- leakance: float32 [15], replicated, may hold values from 0.0005 to 0.02
- well_mask: int32 [16, 2048, 2048], P(None, 'gx', 'gy'), may hold values from 0 to 1, as said below
- rate_index: int32 [2048, 2048], P('gx', 'gy'), may hold values from 0 to 15
- rate_table: float32 [16], replicated, may hold values from 1 to 10
- pit_mask: int32 [16, 2048, 2048], P(None, 'gx', 'gy'), may hold values from 0 to 1, as said below
- pit_level: float32 [16], replicated, may hold values from 1 to 3
Outputs:
- new_drawdown: float32 [16, 2048, 2048], P(None, 'gx', 'gy')
Inputs may be any that keep to these rules, and one draw needn't show every extreme that they name: `pit_mask`: the pit is one box of cells: a rectangle in x and y over the layers from the top down to some depth above the bottom layer. `well_mask`: each well is a column of cells screened over one run of consecutive layers.
All inputs are finite; a program needn't handle non-finite values.
Results may differ from a plain program's by a relative error of at most 0.0023.
Values sent between devices are 32-bit elements; how exact they have to be, the bound alone decides.
A program may use at most 128 MiB of HBM per device.

v0:
```python
import jax
import jax.numpy as jnp
from jax import lax
from jax.experimental import pallas as pl
from jax.experimental.pallas import tpu as pltpu
from jax.sharding import PartitionSpec as P

MESH = pl.DeviceIdType.MESH
HELD = 2.0**100
CELLS = 16
RUNS = 8


def inverse(x):
    return pl.reciprocal(x, approx=True)


def order(count):
    steps = []
    stride = 1
    while stride < count:
        for node in range(stride - 1, count - 1, 2 * stride):
            steps.append((node, node - stride, node + stride))
        stride *= 2
    return steps


def plus(total, term):
    return term if total is None else total + term


def reduce_matrix(c, w):
    c, w, w_left, kept = list(c), list(w), None, {}
    for k, left, right in order(len(c)):
        inv = inverse(w[k] + (c[k] + c[right]))
        tl, tr = c[k] * inv, c[right] * inv
        c[right] = c[k] * tr
        if left < 0:
            w_left = plus(w_left, w[k] * tl)
        else:
            w[left] = w[left] + w[k] * tl
        w[right] = w[right] + w[k] * tr
        kept[k] = (inv, tl, tr)
    return c[-1], w[-1], w_left, kept


def reduce_rhs(b, kept):
    b, b_left, base = list(b), None, {}
    for k, left, right in order(len(b)):
        inv, tl, tr = kept(k)
        if left < 0:
            b_left = plus(b_left, b[k] * tl)
        else:
            b[left] = b[left] + b[k] * tl
        b[right] = b[right] + b[k] * tr
        base[k] = b[k] * inv
    return b[-1], b_left, base


def expand(count, base, tl, tr, s_left, s_last):
    s = {-1: s_left, count - 1: s_last}
    for k, left, right in reversed(order(count)):
        s[k] = base(k) + tl(k) * s[left] + tr(k) * s[right]
    return s


def up(x, by):
    return pltpu.roll(x, RUNS - by, 0)


def down(x, by):
    return pltpu.roll(x, by, 0)


def chain_matrix(c_e, w_e, c_o, w_o, sub):
    inv = inverse(w_e + (c_e + c_o))
    tl, tr = c_e * inv, c_o * inv
    c = c_e * tr
    w = w_o + w_e * tr + jnp.where(sub < RUNS - 1, up(w_e * tl, 1), 0.0)
    kept = [(inv, tl, tr)]
    for by in (1, 2, 4):
        right = jnp.where(sub < RUNS - by, up(c, by), 0.0)
        inv = inverse(w + (c + right))
        tl, tr = c * inv, right * inv
        kept.append((inv, tl, tr))
        w = (
            w
            + jnp.where(sub >= by, down(w * tr, by), 0.0)
            + jnp.where(sub < RUNS - by, up(w * tl, by), 0.0)
        )
        c = jnp.where(sub >= by, down(c * tr, by), c)
    kept.append(inverse(w + c))
    return kept


def chain_rhs(kept, b_e, b_o, sub):
    inv_e, tl_e, tr_e = kept[0]
    b = b_o + b_e * tr_e + jnp.where(sub < RUNS - 1, up(b_e * tl_e, 1), 0.0)
    for by, (inv, tl, tr) in zip((1, 2, 4), kept[1:4]):
        b = (
            b
            + jnp.where(sub >= by, down(b * tr, by), 0.0)
            + jnp.where(sub < RUNS - by, up(b * tl, by), 0.0)
        )
    s_o = b * kept[4]
    s_low = jnp.where(sub >= 1, down(s_o, 1), 0.0)
    s_e = b_e * inv_e + tl_e * s_low + tr_e * s_o
    return s_low, s_e, s_o


def kernel(
    s_in,
    r_in,
    cls_in,
    k_tab,
    leak,
    well_in,
    rate_in,
    rate_tab,
    pit_in,
    level,
    out,
    s_v,
    w_v,
    cls_v,
    well_v,
    rate_v,
    pit_v,
    ra_v,
    rat_v,
    st_v,
    wt_v,
    q_v,
    tmp_v,
    ly_v,
    lz_v,
    fy_v,
    xh_v,
    xl_v,
    xr_v,
    yi_v,
    yl_v,
    yr_v,
    zt_v,
    zi_v,
    ez_v,
    lo_send,
    hi_send,
    x_send,
    lo_recv,
    hi_recv,
    x_recv,
    node_w,
    node_c,
    node_e,
    node_b,
    node_g,
    xa_send,
    xa_recv,
    xb_send,
    xb_recv,
    ym_send,
    ym_recv,
    ya_send,
    ya_recv,
    yb_send,
    yb_recv,
    in_sem,
    out_sem,
    halo_sem,
    a2a_sem,
):
    layers = s_in.shape[0]
    ix, iy = lax.axis_index("gx"), lax.axis_index("gy")
    nx, ny = lax.axis_size("gx"), lax.axis_size("gy")
    rows = RUNS * layers

    loads = [
        pltpu.make_async_copy(src, dst, in_sem.at[n])
        for n, (src, dst) in enumerate(
            [
                (cls_in, cls_v),
                (s_in, s_v),
                (r_in, w_v),
                (pit_in, pit_v),
                (rate_in, rate_v),
                (well_in, well_v),
            ]
        )
    ]
    for load in loads:
        load.start()

    barrier = pltpu.get_barrier_semaphore()

    def greet(k, _):
        pl.semaphore_signal(
            barrier, inc=1, device_id={"gx": lax.rem(ix + k, nx)}, device_id_type=MESH
        )
        return 0

    def greet_y(k, _):
        pl.semaphore_signal(
            barrier, inc=1, device_id={"gy": lax.rem(iy + k, ny)}, device_id_type=MESH
        )
        return 0

    lax.fori_loop(1, nx, greet, 0)
    lax.fori_loop(1, ny, greet_y, 0)

    sub = lax.broadcasted_iota(jnp.int32, (RUNS, 128), 0)
    first, final = sub == 0, sub == RUNS - 1
    ra_tab = [0.5 / jnp.full((RUNS, 128), k_tab[n], jnp.float32) for n in range(8)]
    ra_tab = [jnp.broadcast_to(t[:1], (128, 128)) for t in ra_tab]

    def strided(ref, l):
        return [ref[l, pl.ds(n, RUNS, stride=CELLS), :] for n in range(CELLS)]

    loads[0].wait()
    loads[1].wait()

    def look(l, _):
        cls = cls_v[l]
        odd, two, four = (cls & 1) != 0, (cls & 2) != 0, cls >= 4
        pairs = [jnp.where(odd, ra_tab[n + 1], ra_tab[n]) for n in (0, 2, 4, 6)]
        ra = jnp.where(
            four, jnp.where(two, pairs[3], pairs[2]), jnp.where(two, pairs[1], pairs[0])
        )
        ra_v[l] = ra
        rat_v[l] = ra.T
        st_v[l] = s_v[l].T
        return 0

    lax.fori_loop(0, layers, look, 0)
    lo_send[0] = st_v[:, 0, :]
    lo_send[1] = rat_v[:, 0, :]
    hi_send[0] = st_v[:, 127, :]
    hi_send[1] = rat_v[:, 127, :]
    x_send[...] = ra_v[:, 127, :]

    pl.semaphore_wait(barrier, nx + ny - 2)

    halos = [
        pltpu.make_async_remote_copy(
            src_ref=src,
            dst_ref=dst,
            send_sem=halo_sem.at[2 * n],
            recv_sem=halo_sem.at[2 * n + 1],
            device_id=where,
            device_id_type=MESH,
        )
        for n, (src, dst, where) in enumerate(
            [
                (lo_send, hi_recv, {"gy": lax.rem(iy + ny - 1, ny)}),
                (hi_send, lo_recv, {"gy": lax.rem(iy + 1, ny)}),
                (x_send, x_recv, {"gx": lax.rem(ix + 1, nx)}),
            ]
        )
    ]
    for halo in halos:
        halo.start()

    loads[2].wait()
    loads[3].wait()

    def weigh(l, _):
        pit = pit_v[l] == 1
        w = jnp.where(pit, HELD, inverse(w_v[l]))
        w_v[l] = w
        s_v[l] = w * jnp.where(pit, level[l], s_v[l])
        wt_v[l] = w.T
        return 0

    lax.fori_loop(0, layers, weigh, 0)

    loads[4].wait()
    loads[5].wait()
    rate = rate_v[...]
    pump = jnp.full(rate.shape, rate_tab[0], jnp.float32)
    for n in range(1, 16):
        pump = jnp.where(rate == n, rate_tab[n], pump)
    tmp_v[0] = pump

    for halo in halos:
        halo.wait_recv()
    at_lo, at_hi = iy == 0, iy == ny - 1
    lo_recv[0] = jnp.where(at_lo, 0.0, lo_recv[0])
    lo_recv[1] = jnp.where(at_lo, lo_send[1], lo_recv[1])
    hi_recv[0] = jnp.where(at_hi, 0.0, hi_recv[0])
    hi_recv[1] = jnp.where(at_hi, hi_send[1], hi_recv[1])
    x_recv[...] = jnp.where(ix == 0, ra_v[:, 0, :], x_recv[...])

    ez_v[...] = jnp.zeros_like(ez_v)

    def across(l, _):
        above = jnp.minimum(l + 1, layers - 1)
        below = jnp.maximum(l - 1, 0)
        leak_l = jnp.where(l < layers - 1, leak[jnp.minimum(l, layers - 2)], 0.0)
        leak_b = jnp.where(l > 0, leak[below], 0.0)
        ra, s = strided(rat_v, l), strided(st_v, l)
        ra_left = jnp.where(first, lo_recv[1, pl.ds(l, 1), :], down(ra[15], 1))
        s_left = jnp.where(first, lo_recv[0, pl.ds(l, 1), :], down(s[15], 1))
        face = inverse(ra_left + ra[0])
        fy_v[l, 0] = face
        flux_left = face * (s[0] - s_left)
        face_end = inverse(ra[15] + hi_recv[1, pl.ds(l, 1), :])
        flux_end = face_end * (hi_recv[0, pl.ds(l, 1), :] - s[15])
        flux_end = jnp.where(final, flux_end, up(flux_left, 1))
        flux = flux_left
        for n in range(CELLS):
            if n < CELLS - 1:
                face = inverse(ra[n] + ra[n + 1])
                fy_v[l, n + 1] = face
                flux_next = face * (s[n + 1] - s[n])
            else:
                flux_next = flux_end
            ly = flux_next - flux
            flux = flux_next
            run = pl.ds(n, RUNS, stride=CELLS)
            face_z = leak_l * inverse(ra[n] + rat_v[above, run, :])
            face_b = leak_b * inverse(ra[n] + rat_v[below, run, :])
            lz = face_z * (st_v[above, run, :] - s[n]) - face_b * (s[n] - st_v[below, run, :])
            ly_v[l, n] = ly
            lz_v[l, n] = lz
            tmp_v[1, run, :] = ly + lz
            e = wt_v[l, run, :] + ez_v[n]
            inv = inverse(e + face_z)
            t = face_z * inv
            zt_v[l, n] = t
            zi_v[l, n] = inv
            ez_v[n] = e * t
        q_v[l] = tmp_v[1].T
        return 0

    lax.fori_loop(0, layers, across, 0)

    def whole(ref):
        return ref.at[pl.ds(0, rows - RUNS)]

    def block(ref, n):
        return ref.at[pl.ds(pl.multiple_of(n * RUNS, RUNS), RUNS)]

    def spread(src, dst, pair, axis, me, count):
        def send(k, _):
            other = lax.rem(me + k, count)
            pltpu.make_async_remote_copy(
                src_ref=block(src, other),
                dst_ref=block(dst, me),
                send_sem=a2a_sem.at[2 * pair],
                recv_sem=a2a_sem.at[2 * pair + 1],
                device_id={axis: other},
                device_id_type=MESH,
            ).start()
            return 0

        lax.fori_loop(1, count, send, 0)
        own = pl.ds(pl.multiple_of(me * RUNS, RUNS), RUNS)
        dst[own, :] = src[own, :]

    def arrived(dst, pair):
        pltpu.make_async_copy(whole(dst), whole(dst), a2a_sem.at[2 * pair + 1]).wait()

    def left(src, pair):
        pltpu.make_async_copy(whole(src), whole(src), a2a_sem.at[2 * pair]).wait()

    def nodes(ref, h):
        return [ref[pl.ds(n + 64 * h, 8, stride=RUNS), :] for n in range(RUNS)]

    def put(ref, n, h, x):
        ref[pl.ds(n + 64 * h, 8, stride=RUNS), :] = x

    def join(w, extra):
        return [w[n] + extra[n + 1] for n in range(RUNS - 1)] + [w[RUNS - 1]]

    def runs_x(l, _):
        ra, w = strided(ra_v, l), strided(w_v, l)
        ra_left = jnp.where(first, x_recv[pl.ds(l, 1), :], down(ra[15], 1))
        c = [inverse(ra_left + ra[0])]
        c += [inverse(ra[n] + ra[n + 1]) for n in range(CELLS - 1)]
        b = []
        for n in range(CELLS):
            run = pl.ds(n, RUNS, stride=CELLS)
            pumped = well_v[l, run, :].astype(jnp.float32) * tmp_v[0, run, :]
            b.append(s_v[l, run, :] + (q_v[l, run, :] + pumped))
        c, w, e, kept = reduce_matrix(c, w)
        b, g, base = reduce_rhs(b, lambda k: kept[k])
        for k in base:
            xh_v[l, k] = base[k]
            xl_v[l, k] = kept[k][1]
            xr_v[l, k] = kept[k][2]
        at = pl.ds(pl.multiple_of(l * RUNS, RUNS), RUNS)
        for ref, x in ((node_w, w), (node_c, c), (node_e, e), (node_b, b), (node_g, g)):
            ref[at, :] = x
        return 0

    lax.fori_loop(0, layers, runs_x, 0)

    x_runs = []
    for h in range(2):
        w_extra, b_extra = nodes(node_e, h), nodes(node_g, h)
        c, w, e, kept = reduce_matrix(nodes(node_c, h), join(nodes(node_w, h), w_extra))
        b, g, base = reduce_rhs(join(nodes(node_b, h), b_extra), lambda k: kept[k])
        edge = inverse(2.0 * x_send[pl.ds(8 * h, 8), :])
        w = w + jnp.where(ix == nx - 1, edge, 0.0)
        for n, x in enumerate((c, w, e + w_extra[0], b, g + b_extra[0])):
            put(xa_send, n, h, x)
        x_runs.append((base, kept))
    spread(xa_send, xa_recv, 0, "gx", ix, nx)

    def runs_y(l, _):
        c = [fy_v[l, n] for n in range(CELLS)]
        c, w, e, kept = reduce_matrix(c, strided(wt_v, l))
        for k in kept:
            yi_v[l, k], yl_v[l, k], yr_v[l, k] = kept[k]
        at = pl.ds(pl.multiple_of(l * RUNS, RUNS), RUNS)
        for ref, x in ((node_w, w), (node_c, c), (node_e, e)):
            ref[at, :] = x
        return 0

    lax.fori_loop(0, layers, runs_y, 0)

    y_runs = []
    for h in range(2):
        w_extra = nodes(node_e, h)
        c, w, e, kept = reduce_matrix(nodes(node_c, h), join(nodes(node_w, h), w_extra))
        edge = inverse(2.0 * hi_send[1, pl.ds(8 * h, 8), :])
        w = w + jnp.where(iy == ny - 1, edge, 0.0)
        for n, x in enumerate((c, w, e + w_extra[0])):
            put(ym_send, n, h, x)
        y_runs.append(kept)
    spread(ym_send, ym_recv, 2, "gy", iy, ny)

    def take(ref, n):
        even = ref[pl.ds(n, 8, stride=2 * RUNS), :]
        odd = ref[pl.ds(RUNS + n, 8, stride=2 * RUNS), :]
        return even, odd

    def beyond(odd_w, extra_e):
        return odd_w + jnp.where(final, 0.0, up(extra_e, 1))

    def give(ref, s_low, s_e, s_o):
        ref[pl.ds(0, 8, stride=2 * RUNS), :] = s_low
        ref[pl.ds(1, 8, stride=2 * RUNS), :] = s_e
        ref[pl.ds(RUNS, 8, stride=2 * RUNS), :] = s_e
        ref[pl.ds(RUNS + 1, 8, stride=2 * RUNS), :] = s_o

    arrived(xa_recv, 0)
    c, w, e, b, g = [take(xa_recv, n) for n in range(5)]
    kept = chain_matrix(c[0], w[0] + e[1], c[1], beyond(w[1], e[0]), sub)
    give(xb_send, *chain_rhs(kept, b[0] + g[1], beyond(b[1], g[0]), sub))
    spread(xb_send, xb_recv, 1, "gx", ix, nx)

    arrived(ym_recv, 2)
    c, w, e = [take(ym_recv, n) for n in range(3)]
    y_chain = chain_matrix(c[0], w[0] + e[1], c[1], beyond(w[1], e[0]), sub)

    arrived(xb_recv, 1)

    def ends(ref, h, base, kept):
        s_left = ref[pl.ds(64 * h, 8, stride=RUNS), :]
        s_last = ref[pl.ds(64 * h + 1, 8, stride=RUNS), :]
        s = expand(
            RUNS, lambda k: base[k], lambda k: kept[k][1], lambda k: kept[k][2], s_left, s_last
        )
        for n in range(RUNS):
            put(node_w, n, h, s[n])
            put(node_c, n, h, s[n - 1])

    for h in range(2):
        ends(xb_recv, h, *x_runs[h])

    def fill_x(l, _):
        at = pl.ds(pl.multiple_of(l * RUNS, RUNS), RUNS)
        s = expand(
            CELLS,
            lambda k: xh_v[l, k],
            lambda k: xl_v[l, k],
            lambda k: xr_v[l, k],
            node_c[at, :],
            node_w[at, :],
        )
        for n in range(CELLS):
            tmp_v[1, pl.ds(n, RUNS, stride=CELLS), :] = s[n]
        q_v[l] = tmp_v[1].T
        b = []
        for n in range(CELLS):
            run = pl.ds(n, RUNS, stride=CELLS)
            b.append(wt_v[l, run, :] * q_v[l, run, :] - ly_v[l, n])
        b, g, base = reduce_rhs(b, lambda k: (yi_v[l, k], yl_v[l, k], yr_v[l, k]))
        for k in base:
            xh_v[l, k] = base[k]
        node_b[at, :] = b
        node_g[at, :] = g
        return 0

    lax.fori_loop(0, layers, fill_x, 0)

    y_base = []
    for h in range(2):
        b_extra = nodes(node_g, h)
        b, g, base = reduce_rhs(join(nodes(node_b, h), b_extra), lambda k: y_runs[h][k])
        put(ya_send, 0, h, b)
        put(ya_send, 1, h, g + b_extra[0])
        y_base.append(base)
    spread(ya_send, ya_recv, 3, "gy", iy, ny)
    arrived(ya_recv, 3)
    b, g = take(ya_recv, 0), take(ya_recv, 1)
    give(yb_send, *chain_rhs(y_chain, b[0] + g[1], beyond(b[1], g[0]), sub))
    spread(yb_send, yb_recv, 4, "gy", iy, ny)
    arrived(yb_recv, 4)
    for h in range(2):
        ends(yb_recv, h, y_base[h], y_runs[h])

    ez_v[...] = jnp.zeros_like(ez_v)

    def fill_y(l, _):
        at = pl.ds(pl.multiple_of(l * RUNS, RUNS), RUNS)
        s = expand(
            CELLS,
            lambda k: xh_v[l, k],
            lambda k: yl_v[l, k],
            lambda k: yr_v[l, k],
            node_c[at, :],
            node_w[at, :],
        )
        for n in range(CELLS):
            b = wt_v[l, pl.ds(n, RUNS, stride=CELLS), :] * s[n] - lz_v[l, n] + ez_v[n]
            ez_v[n] = b * zt_v[l, n]
            zi_v[l, n] = b * zi_v[l, n]
        return 0

    lax.fori_loop(0, layers, fill_y, 0)

    ez_v[...] = jnp.zeros_like(ez_v)

    def write(l, _):
        return pltpu.make_async_copy(q_v.at[l], out.at[l], out_sem)

    def fill_z(step, _):
        l = layers - 1 - step
        for n in range(CELLS):
            s = zi_v[l, n] + zt_v[l, n] * ez_v[n]
            ez_v[n] = s
            tmp_v[1, pl.ds(n, RUNS, stride=CELLS), :] = s
        q_v[l] = tmp_v[1].T
        return 0

    lax.fori_loop(0, layers, fill_z, 0)
    final_copy = pltpu.make_async_copy(q_v, out, out_sem)
    final_copy.start()
    for halo in halos:
        halo.wait_send()
    left(xa_send, 0)
    left(xb_send, 1)
    left(ym_send, 2)
    left(ya_send, 3)
    left(yb_send, 4)
    final_copy.wait()


def body(*args):
    layers, cells_x, cells_y = args[0].shape
    field = pltpu.VMEM((layers, cells_x, cells_y), jnp.float32)
    index = pltpu.VMEM((layers, cells_x, cells_y), jnp.int32)
    runs = pltpu.VMEM((layers, CELLS, RUNS, 128), jnp.float32)
    rows = pltpu.VMEM((RUNS * layers, 128), jnp.float32)
    halo = pltpu.VMEM((2, layers, 128), jnp.float32)
    edge = pltpu.VMEM((layers, 128), jnp.float32)
    hbm = pl.BlockSpec(memory_space=pl.ANY)
    smem = pl.BlockSpec(memory_space=pltpu.SMEM)
    return pl.pallas_call(
        kernel,
        out_shape=jax.ShapeDtypeStruct(args[0].shape, jnp.float32),
        in_specs=[hbm, hbm, hbm, smem, smem, hbm, hbm, smem, hbm, smem],
        out_specs=hbm,
        scratch_shapes=[
            field,
            field,
            index,
            index,
            pltpu.VMEM((cells_x, cells_y), jnp.int32),
            index,
            field,
            field,
            field,
            field,
            field,
            pltpu.VMEM((2, cells_x, cells_y), jnp.float32),
            runs,
            runs,
            runs,
            runs,
            runs,
            runs,
            runs,
            runs,
            runs,
            runs,
            runs,
            pltpu.VMEM((CELLS, RUNS, 128), jnp.float32),
            halo,
            halo,
            edge,
            halo,
            halo,
            edge,
        ]
        + [rows] * 15
        + [
            pltpu.SemaphoreType.DMA((6,)),
            pltpu.SemaphoreType.DMA,
            pltpu.SemaphoreType.DMA((6,)),
            pltpu.SemaphoreType.DMA((10,)),
        ],
        compiler_params=pltpu.CompilerParams(
            collective_id=0, has_side_effects=True, vmem_limit_bytes=56 * 1024 * 1024
        ),
        cost_estimate=pl.CostEstimate(
            flops=100 * args[0].size, bytes_accessed=24 * args[0].size, transcendentals=0
        ),
        name="drawdown_step",
    )(*args)


def solution(mesh):
    field = P(None, "gx", "gy")
    in_specs = (field, field, field, P(), P(), field, P("gx", "gy"), P(), field, P())
    return jax.shard_map(body, mesh=mesh, in_specs=in_specs, out_specs=field, check_vma=False)
```

profile of v0, /device:TPU:1, one launch (start us, length us, event | category | flops | bytes accessed | tf_op | source)
XLA Modules:
  0.0 50.6 jit_solution(13783442468687913113)
XLA Ops:
  0.0 48.3 %drawdown_step.1 = f32[16,128,128]{2,1,0:T(8,128)} custom-call(f32[16,128,128]{2,1,0:T(8,128)} %s_in.1, f32[16,128,128]{2,1,0:T(8,128)} %r_in.1, s32[16,128,128]{2,1,0:T(8,128)} %cls_in.1, f32[8]{0:T(128)} %k_tab.1, f32[15]{0:T(128)} %leak.1, s32[16,128,128]{2,1,0:T(8,128)} %well_in.1, s32[128,128]{1,0:T(8,128)} %rate_in.1, f32[16]{0:T(128)} %rate_tab.1, ...), custom_call_target="tpu_custom_call" | custom-call | flops 26214400 | bytes 6291456 | tf_op jit(solution)/shard_map/drawdown_step/pallas_call | solution.py:571
  48.3 2.3 %copy.12 = f32[16,128,128]{2,1,0:T(8,128)} copy(f32[16,128,128]{2,1,0:T(8,128)} %drawdown_step.1) | data formatting | bytes 2097152
where the time goes:
time: 50.8 us; the launch traced here: 50.6 us
  Pallas kernels  48.3 us (95%)
  local copies, waits for them, and re-layouts  2.3 us (5%)
    pallas_call x1, Pallas kernels, body(): pl.pallas_call(kernel, out_shape=jax.ShapeDtypeStruct(args[0].shape, jnp....  48.3 us
    unnamed x1, local copies, waits for them, and re-layouts  2.3 us

commit v1 on v0

v1 whole, which is shorter than its diff:
```python
import jax
import jax.numpy as jnp
from jax import lax
from jax.experimental import pallas as pl
from jax.experimental.pallas import tpu as pltpu
from jax.sharding import PartitionSpec as P

MESH = pl.DeviceIdType.MESH
HELD = 2.0**100
CELLS = 16
RUNS = 8
TILE = CELLS * RUNS


def inverse(x):
    return pltpu.reciprocal(x, approx=True)


def order(count):
    steps = []
    stride = 1
    while stride < count:
        for node in range(stride - 1, count - 1, 2 * stride):
            steps.append((node, node - stride, node + stride))
        stride *= 2
    return steps


def plus(total, term):
    return term if total is None else total + term


def reduce_matrix(c, w):
    c, w, w_left, kept = list(c), list(w), None, {}
    for k, left, right in order(len(c)):
        inv = inverse(w[k] + (c[k] + c[right]))
        tl, tr = c[k] * inv, c[right] * inv
        c[right] = c[k] * tr
        if left < 0:
            w_left = plus(w_left, w[k] * tl)
        else:
            w[left] = w[left] + w[k] * tl
        w[right] = w[right] + w[k] * tr
        kept[k] = (inv, tl, tr)
    return c[-1], w[-1], w_left, kept


def reduce_rhs(b, kept):
    b, b_left, base = list(b), None, {}
    for k, left, right in order(len(b)):
        inv, tl, tr = kept(k)
        if left < 0:
            b_left = plus(b_left, b[k] * tl)
        else:
            b[left] = b[left] + b[k] * tl
        b[right] = b[right] + b[k] * tr
        base[k] = b[k] * inv
    return b[-1], b_left, base


def expand(count, base, tl, tr, s_left, s_last):
    s = {-1: s_left, count - 1: s_last}
    for k, left, right in reversed(order(count)):
        s[k] = base(k) + tl(k) * s[left] + tr(k) * s[right]
    return s


def take_out(c_left, c_right, w):
    inv = inverse(w + (c_left + c_right))
    tl, tr = c_left * inv, c_right * inv
    return c_left * tr, w * tl, w * tr, (inv, tl, tr)


def down(x):
    return pltpu.roll(x, 1, 0)


def up(x):
    return pltpu.roll(x, RUNS - 1, 0)


def looped(count, unroll, step):
    def body(i, _):
        step([i * unroll + u for u in range(unroll)])
        return 0

    lax.fori_loop(0, count // unroll, body, 0)


def runs_kernel(
    s_in,
    r_in,
    cls_in,
    k_tab,
    leak,
    well_in,
    rate_in,
    rate_tab,
    pit_in,
    level,
    zi_out,
    zt_out,
    s_v,
    w_v,
    cls_v,
    well_v,
    rate_v,
    pit_v,
    ra_v,
    xi_v,
    xl_v,
    xr_v,
    rat_v,
    st_v,
    wt_v,
    q_v,
    wr_v,
    ly_v,
    lz_v,
    fy_v,
    yi_v,
    yl_v,
    yr_v,
    zt_v,
    zi_v,
    pump_v,
    ez_v,
    flux_v,
    ra_c,
    s_c,
    lo_send,
    hi_send,
    lo_recv,
    hi_recv,
    node_w,
    node_c,
    node_e,
    node_b,
    node_g,
    xm_send,
    xm_recv,
    xr_send,
    xr_recv,
    xs_v,
    pm_send,
    pm_recv,
    ym_send,
    ym_recv,
    pr_send,
    pr_recv,
    yr_send,
    yr_recv,
    ys_v,
    pb_send,
    pb_recv,
    yl_end,
    yr_end,
    in_sem,
    out_sem,
    send_sem,
    recv_sem,
):
    layers = s_in.shape[0]
    ix, iy = lax.axis_index("gx"), lax.axis_index("gy")
    nx, ny = lax.axis_size("gx"), lax.axis_size("gy")
    core, chip = lax.rem(iy, 2), iy // 2
    mate = {"gy": iy + 1 - 2 * core}
    halves = range(layers // 8)

    fields = [(cls_in, cls_v), (s_in, s_v), (r_in, w_v), (pit_in, pit_v), (well_in, well_v)]
    for n, (src, dst) in enumerate(fields):
        for q in range(RUNS):
            pltpu.make_async_copy(
                src.at[:, pl.ds(CELLS * q, CELLS), :], dst.at[:, :, q, :], in_sem.at[n]
            ).start()
    for q in range(RUNS):
        pltpu.make_async_copy(
            rate_in.at[pl.ds(CELLS * q, CELLS), :], rate_v.at[:, q, :], in_sem.at[5]
        ).start()

    def loaded(n):
        ref = fields[n][1] if n < 5 else rate_v
        pltpu.make_async_copy(ref, ref, in_sem.at[n]).wait()

    barrier = pltpu.get_barrier_semaphore()

    def greet(where):
        pl.semaphore_signal(barrier, inc=1, device_id=where, device_id_type=MESH)

    def greet_x(k, _):
        greet({"gx": lax.rem(ix + k, nx)})
        return 0

    def greet_y(k, _):
        greet({"gy": lax.rem(iy + 2 * k, ny)})
        return 0

    lax.fori_loop(1, nx, greet_x, 0)
    lax.fori_loop(1, ny // 2, greet_y, 0)
    greet({"gy": lax.rem(iy + 1, ny)})
    greet({"gy": lax.rem(iy + ny - 1, ny)})

    def remote(src, dst, n, where):
        return pltpu.make_async_remote_copy(
            src_ref=src,
            dst_ref=dst,
            send_sem=send_sem.at[n],
            recv_sem=recv_sem.at[n],
            device_id=where,
            device_id_type=MESH,
        )

    sub = lax.broadcasted_iota(jnp.int32, (RUNS, 128), 0)
    first, final = sub == 0, sub == RUNS - 1

    def at(l):
        return pl.ds(pl.multiple_of(l * RUNS, RUNS), RUNS)

    def turned(x):
        return x.reshape(TILE, 128).T

    def strided(ref, l):
        return [ref[l, pl.ds(n, RUNS, stride=CELLS), :] for n in range(CELLS)]

    ra_tab = [0.5 / jnp.full((RUNS, 128), k_tab[n], jnp.float32) for n in range(8)]
    ra_tab = [jnp.broadcast_to(t[:1], (TILE, 128)).reshape(CELLS, RUNS, 128) for t in ra_tab]
    loaded(0)
    loaded(1)

    def look(ls):
        ras = []
        for l in ls:
            cls = cls_v[l]
            odd, two, four = (cls & 1) != 0, (cls & 2) != 0, cls >= 4
            pairs = [jnp.where(odd, ra_tab[n + 1], ra_tab[n]) for n in (0, 2, 4, 6)]
            ras.append(
                jnp.where(
                    four,
                    jnp.where(two, pairs[3], pairs[2]),
                    jnp.where(two, pairs[1], pairs[0]),
                )
            )
        ss = [s_v[l] for l in ls]
        turned_ra = [turned(x) for x in ras]
        turned_s = [turned(x) for x in ss]
        for u, l in enumerate(ls):
            ra_v[l] = ras[u]
            rat_v[l] = turned_ra[u]
            st_v[l] = turned_s[u]

    looped(layers, 4, look)
    lo_send[0] = st_v[:, 0, :]
    lo_send[1] = rat_v[:, 0, :]
    hi_send[0] = st_v[:, TILE - 1, :]
    hi_send[1] = rat_v[:, TILE - 1, :]

    pl.semaphore_wait(barrier, nx + ny // 2)
    halos = [
        remote(lo_send, hi_recv, 0, {"gy": lax.rem(iy + ny - 1, ny)}),
        remote(hi_send, lo_recv, 1, {"gy": lax.rem(iy + 1, ny)}),
    ]
    for halo in halos:
        halo.start()

    loaded(2)
    loaded(3)
    own_x = jnp.where(ix == 0, 1.0, 0.0)

    def weigh(ls):
        ws = []
        for l in ls:
            pit = pit_v[l] == 1
            w = jnp.where(pit, HELD, inverse(w_v[l]))
            ws.append(w)
            s_v[l] = w * jnp.where(pit, level[l], s_v[l])
        wts = [turned(w) for w in ws]
        for u, l in enumerate(ls):
            wt_v[l] = wts[u]
        for u, l in enumerate(ls):
            ra, w = [ra_v[l, n] for n in range(CELLS)], [ws[u][n] for n in range(CELLS)]
            w_v[l] = ws[u]
            c = [inverse(ra[0] + jnp.where(first, own_x * ra[0], down(ra[15])))]
            c += [inverse(ra[n] + ra[n + 1]) for n in range(CELLS - 1)]
            c, w, e, kept = reduce_matrix(c, w)
            for k in kept:
                xi_v[l, k], xl_v[l, k], xr_v[l, k] = kept[k]
            node_w[at(l), :], node_c[at(l), :], node_e[at(l), :] = w, c, e

    looped(layers, 2, weigh)

    def nodes(ref, h):
        return [ref[pl.ds(n + 64 * h, 8, stride=RUNS), :] for n in range(RUNS)]

    def put(ref, n, h, x):
        ref[pl.ds(n + 64 * h, 8, stride=RUNS), :] = x

    def join(w, extra):
        return [w[n] + extra[n + 1] for n in range(RUNS - 1)] + [w[RUNS - 1]]

    def segment(h, c_end):
        extra = nodes(node_e, h)
        c, w, e, kept = reduce_matrix(nodes(node_c, h), join(nodes(node_w, h), extra))
        c, w_left, w_right, last = take_out(c, c_end, w)
        kept[RUNS - 1] = last
        return (c, extra[0] + e + w_left, w_right), kept

    def segment_rhs(h, kept):
        extra = nodes(node_g, h)
        b, g, base = reduce_rhs(join(nodes(node_b, h), extra), lambda k: kept[k])
        inv, tl, tr = kept[RUNS - 1]
        base[RUNS - 1] = b * inv
        return (extra[0] + g + b * tl, b * tr), base

    x_kept = []
    end_x = jnp.where(ix == nx - 1, 2.0, 1.0)
    for h in halves:
        values, kept = segment(h, inverse(end_x * ra_v[pl.ds(8 * h, 8), CELLS - 1, RUNS - 1, :]))
        for n, x in enumerate(values):
            xm_send[pl.ds(layers * n + 8 * h, 8), :] = x
        x_kept.append(kept)

    def gather_x(src, dst, n):
        def send(k, _):
            other = lax.rem(ix + k, nx)
            remote(src, dst.at[ix], n, {"gx": other}).start()
            return 0

        lax.fori_loop(1, nx, send, 0)
        dst[ix] = src[...]

    def gather_y(src, dst, n):
        def send(k, _):
            other = lax.rem(iy + 2 * k, ny)
            remote(src, dst.at[chip], n, {"gy": other}).start()
            return 0

        lax.fori_loop(1, ny // 2, send, 0)
        dst[chip] = src[...]

    def arrived(dst, n, count):
        ref = dst.at[pl.ds(0, count)]
        pltpu.make_async_copy(ref, ref, recv_sem.at[n]).wait()

    gather_x(xm_send, xm_recv, 2)

    ez_v[...] = jnp.zeros_like(ez_v)
    flux_v[...] = jnp.zeros_like(flux_v)
    own_y = jnp.where(iy == 0, 1.0, 0.0)
    for n in range(CELLS):
        ra_c[n] = rat_v[0, pl.ds(n, RUNS, stride=CELLS), :]
        s_c[n] = st_v[0, pl.ds(n, RUNS, stride=CELLS), :]

    def across(ls):
        ra = [ra_c[n] for n in range(CELLS)]
        s = [s_c[n] for n in range(CELLS)]
        for l in ls:
            above = jnp.minimum(l + 1, layers - 1)
            leak_l = jnp.where(l < layers - 1, leak[jnp.minimum(l, layers - 2)], 0.0)
            ra_up, s_up = strided(rat_v, above), strided(st_v, above)
            wt = strided(wt_v, l)
            ra_before = down(ra[15])
            face = inverse(ra[0] + jnp.where(first, own_y * ra[0], ra_before))
            fy_v[l, 0] = face
            flux_left = jnp.where(first, 0.0, face * (s[0] - down(s[15])))
            flux = flux_left
            for n in range(CELLS):
                if n < CELLS - 1:
                    face = inverse(ra[n] + ra[n + 1])
                    fy_v[l, n + 1] = face
                    flux_next = face * (s[n + 1] - s[n])
                else:
                    flux_next = up(flux_left)
                ly = flux_next - flux
                flux = flux_next
                face_z = leak_l * inverse(ra[n] + ra_up[n])
                flux_z = face_z * (s_up[n] - s[n])
                lz = flux_z - flux_v[n]
                flux_v[n] = flux_z
                ly_v[l, n] = ly
                lz_v[l, n] = lz
                q_v[l, pl.ds(n, RUNS, stride=CELLS), :] = ly + lz
                wr_v[l, n] = wt[n]
                e = wt[n] + ez_v[n]
                inv = inverse(e + face_z)
                t = face_z * inv
                zt_v[l, n] = t
                zi_v[l, n] = inv
                ez_v[n] = e * t
            ra, s = ra_up, s_up
        for n in range(CELLS):
            ra_c[n], s_c[n] = ra[n], s[n]

    looped(layers, 2, across)
    zt_copy = pltpu.make_async_copy(zt_v, zt_out, out_sem.at[0])
    zt_copy.start()

    loaded(4)
    loaded(5)
    rate = rate_v[...]
    pump = jnp.full(rate.shape, rate_tab[0], jnp.float32)
    for n in range(1, 16):
        pump = jnp.where(rate == n, rate_tab[n], pump)
    pump_v[...] = pump

    for halo in halos:
        halo.wait_recv()
    at_lo, at_hi = iy == 0, iy == ny - 1
    s_lo = jnp.where(at_lo, 0.0, lo_recv[0])
    ra_lo = jnp.where(at_lo, lo_send[1], lo_recv[1])
    s_hi = jnp.where(at_hi, 0.0, hi_recv[0])
    ra_hi = jnp.where(at_hi, hi_send[1], hi_recv[1])
    flux_lo = inverse(ra_lo + lo_send[1]) * (lo_send[0] - s_lo)
    flux_hi = inverse(ra_hi + hi_send[1]) * (s_hi - hi_send[0])
    q_v[:, 0, :] = q_v[:, 0, :] - flux_lo
    q_v[:, TILE - 1, :] = q_v[:, TILE - 1, :] + flux_hi
    ly_v[:, 0, 0, :] = ly_v[:, 0, 0, :] - flux_lo
    ly_v[:, CELLS - 1, RUNS - 1, :] = ly_v[:, CELLS - 1, RUNS - 1, :] + flux_hi

    def runs_x(ls):
        qs = [q_v[l].T.reshape(CELLS, RUNS, 128) for l in ls]
        bs = []
        for u, l in enumerate(ls):
            pumped = well_v[l].astype(jnp.float32) * pump_v[...]
            bs.append(s_v[l] + (qs[u] + pumped))
        for u, l in enumerate(ls):
            b, g, base = reduce_rhs(
                [bs[u][n] for n in range(CELLS)], lambda k: (xi_v[l, k], xl_v[l, k], xr_v[l, k])
            )
            for k in base:
                xi_v[l, k] = base[k]
            node_b[at(l), :], node_g[at(l), :] = b, g

    looped(layers, 4, runs_x)

    x_base = []
    for h in halves:
        values, base = segment_rhs(h, x_kept[h])
        for n, x in enumerate(values):
            xr_send[pl.ds(layers * n + 8 * h, 8), :] = x
        x_base.append(base)
    gather_x(xr_send, xr_recv, 3)

    def runs_y(ls):
        for l in ls:
            c, w, e, kept = reduce_matrix(
                [fy_v[l, n] for n in range(CELLS)], [wr_v[l, n] for n in range(CELLS)]
            )
            for k in kept:
                yi_v[l, k], yl_v[l, k], yr_v[l, k] = kept[k]
            node_w[at(l), :], node_c[at(l), :], node_e[at(l), :] = w, c, e

    looped(layers, 2, runs_y)

    is_a = core == 0

    def mine(pair):
        return jnp.where(is_a, pair[0], pair[1])

    def theirs(pair):
        return jnp.where(is_a, pair[1], pair[0])

    y_kept, y_values = [], []
    end_y = jnp.where(iy == ny - 1, 2.0, 1.0)
    for h in halves:
        values, kept = segment(h, inverse(end_y * hi_send[1, pl.ds(8 * h, 8), :]))
        y_values.append(values)
        y_kept.append(kept)
    for n, pair in enumerate(zip(*y_values)):
        pm_send[pl.ds(8 * n, 8), :] = theirs(pair)
    pm_copy = remote(pm_send, pm_recv, 4, mate)
    pm_copy.start()
    own = [mine(pair) for pair in zip(*y_values)]
    pm_copy.wait_recv()
    other = [pm_recv[pl.ds(8 * n, 8), :] for n in range(3)]
    c_a, c_b = mine((own[0], other[0])), theirs((own[0], other[0]))
    el_a, el_b = mine((own[1], other[1])), theirs((own[1], other[1]))
    er_a, er_b = mine((own[2], other[2])), theirs((own[2], other[2]))
    c, w_left, w_right, mid = take_out(c_a, c_b, er_a + el_b)
    for n, x in enumerate((c, el_a + w_left, er_b + w_right)):
        ym_send[pl.ds(8 * n, 8), :] = x
    gather_y(ym_send, ym_recv, 5)

    arrived(xm_recv, 2, nx - 1)
    zero = jnp.zeros((RUNS, 128), jnp.float32)

    def rows(ref, d, n, h):
        return ref[d, pl.ds(layers * n + 8 * h, 8), :]

    x_chain = []
    for h in halves:
        c = [rows(xm_recv, d, 0, h) for d in range(nx)]
        w = [rows(xm_recv, d, 2, h) + rows(xm_recv, d + 1, 1, h) for d in range(nx - 1)]
        x_chain.append(reduce_matrix(c, w + [zero])[3])

    arrived(xr_recv, 3, nx - 1)
    for h in halves:
        kept = x_chain[h]
        b = [rows(xr_recv, d, 1, h) + rows(xr_recv, d + 1, 0, h) for d in range(nx - 1)]
        base = reduce_rhs(b + [zero], lambda k: kept[k])[2]
        s = expand(
            nx, lambda k: base[k], lambda k: kept[k][1], lambda k: kept[k][2], zero, zero
        )
        for d in range(-1, nx):
            xs_v[d + 1, pl.ds(8 * h, 8), :] = s[d]

    def ends(s_left, s_right, h, base, kept):
        inv, tl, tr = kept[RUNS - 1]
        s_last = base[RUNS - 1] + tl * s_left + tr * s_right
        s = expand(
            RUNS, lambda k: base[k], lambda k: kept[k][1], lambda k: kept[k][2], s_left, s_last
        )
        for n in range(RUNS):
            put(node_w, n, h, s[n])
            put(node_c, n, h, s[n - 1])

    for h in halves:
        part = pl.ds(8 * h, 8)
        ends(xs_v[ix, part, :], xs_v[ix + 1, part, :], h, x_base[h], x_kept[h])

    def fill(l, base, tl, tr):
        s = expand(
            CELLS,
            lambda k: base[l, k],
            lambda k: tl[l, k],
            lambda k: tr[l, k],
            node_c[at(l), :],
            node_w[at(l), :],
        )
        return [s[n] for n in range(CELLS)]

    def fill_x(ls):
        lines = [turned(jnp.stack(fill(l, xi_v, xl_v, xr_v))) for l in ls]
        for u, l in enumerate(ls):
            q_v[l] = lines[u]
        for l in ls:
            sx = strided(q_v, l)
            b = [wr_v[l, n] * sx[n] - ly_v[l, n] for n in range(CELLS)]
            b, g, base = reduce_rhs(b, lambda k: (yi_v[l, k], yl_v[l, k], yr_v[l, k]))
            for k in base:
                yi_v[l, k] = base[k]
            node_b[at(l), :], node_g[at(l), :] = b, g

    looped(layers, 4, fill_x)

    y_base, y_values = [], []
    for h in halves:
        values, base = segment_rhs(h, y_kept[h])
        y_values.append(values)
        y_base.append(base)
    for n, pair in enumerate(zip(*y_values)):
        pr_send[pl.ds(8 * n, 8), :] = theirs(pair)
    pr_copy = remote(pr_send, pr_recv, 6, mate)
    pr_copy.start()
    own = [mine(pair) for pair in zip(*y_values)]

    arrived(ym_recv, 5, ny // 2 - 1)
    chips = ny // 2
    c = [ym_recv[d, pl.ds(0, 8), :] for d in range(chips)]
    w = [ym_recv[d, pl.ds(16, 8), :] + ym_recv[d + 1, pl.ds(8, 8), :] for d in range(chips - 1)]
    y_chain = reduce_matrix(c, w + [zero])[3]

    pr_copy.wait_recv()
    other = [pr_recv[pl.ds(8 * n, 8), :] for n in range(2)]
    gl_a, gl_b = mine((own[0], other[0])), theirs((own[0], other[0]))
    gr_a, gr_b = mine((own[1], other[1])), theirs((own[1], other[1]))
    b_mid = gr_a + gl_b
    inv_mid, tl_mid, tr_mid = mid
    yr_send[pl.ds(0, 8), :] = gl_a + b_mid * tl_mid
    yr_send[pl.ds(8, 8), :] = gr_b + b_mid * tr_mid
    gather_y(yr_send, yr_recv, 7)
    arrived(yr_recv, 7, chips - 1)
    b = [yr_recv[d, pl.ds(8, 8), :] + yr_recv[d + 1, pl.ds(0, 8), :] for d in range(chips - 1)]
    base = reduce_rhs(b + [zero], lambda k: y_chain[k])[2]
    s = expand(
        chips, lambda k: base[k], lambda k: y_chain[k][1], lambda k: y_chain[k][2], zero, zero
    )
    for d in range(-1, chips):
        ys_v[d + 1] = s[d]
    s_left, s_right = ys_v[chip], ys_v[chip + 1]
    s_mid = b_mid * inv_mid + tl_mid * s_left + tr_mid * s_right
    pb_send[pl.ds(0, 8), :] = theirs((s_left, s_mid))
    pb_send[pl.ds(8, 8), :] = theirs((s_mid, s_right))
    pb_copy = remote(pb_send, pb_recv, 8, mate)
    pb_copy.start()
    yl_end[at(core), :] = mine((s_left, s_mid))
    yr_end[at(core), :] = mine((s_mid, s_right))
    pb_copy.wait_recv()
    yl_end[at(1 - core), :] = pb_recv[pl.ds(0, 8), :]
    yr_end[at(1 - core), :] = pb_recv[pl.ds(8, 8), :]
    for h in halves:
        part = pl.ds(8 * h, 8)
        ends(yl_end[part, :], yr_end[part, :], h, y_base[h], y_kept[h])

    ez_v[...] = jnp.zeros_like(ez_v)

    def fill_y(ls):
        lines = [fill(l, yi_v, yl_v, yr_v) for l in ls]
        for u, l in enumerate(ls):
            for n in range(CELLS):
                b = wr_v[l, n] * lines[u][n] - lz_v[l, n] + ez_v[n]
                ez_v[n] = b * zt_v[l, n]
                zi_v[l, n] = b * zi_v[l, n]
            pltpu.make_async_copy(zi_v.at[l], zi_out.at[l], out_sem.at[1]).start()

    looped(layers, 2, fill_y)

    for halo in halos:
        halo.wait_send()
    for copy in (pm_copy, pr_copy, pb_copy):
        copy.wait_send()
    for ref, n, count in ((xm_recv, 2, nx), (xr_recv, 3, nx), (ym_recv, 5, chips), (yr_recv, 7, chips)):
        sent = ref.at[pl.ds(0, count - 1)]
        pltpu.make_async_copy(sent, sent, send_sem.at[n]).wait()
    zt_copy.wait()
    pltpu.make_async_copy(zi_v, zi_out, out_sem.at[1]).wait()


def layers_kernel(zi_in, zt_in, out, zi_v, zt_v, tmp_v, out_v, ez_v, in_sem, out_sem):
    layers = zi_in.shape[0]
    group = 4
    parts = list(range(layers - group, -1, -group))
    loads = []
    for n, l in enumerate(parts):
        part = pl.ds(l, group)
        loads.append(
            [
                pltpu.make_async_copy(zi_in.at[part], zi_v.at[part], in_sem.at[2 * n]),
                pltpu.make_async_copy(zt_in.at[part], zt_v.at[part], in_sem.at[2 * n + 1]),
            ]
        )
        for load in loads[-1]:
            load.start()
    ez_v[...] = jnp.zeros_like(ez_v)
    for n, l0 in enumerate(parts):
        for load in loads[n]:
            load.wait()
        for l in range(l0 + group - 1, l0 - 1, -1):
            for k in range(CELLS):
                s = zi_v[l, k] + zt_v[l, k] * ez_v[k]
                ez_v[k] = s
                tmp_v[l - l0, pl.ds(k, RUNS, stride=CELLS), :] = s
        for l in range(l0 + group - 1, l0 - 1, -1):
            out_v[l] = tmp_v[l - l0].T.reshape(CELLS, RUNS, 128)
        for q in range(RUNS):
            pltpu.make_async_copy(
                out_v.at[pl.ds(l0, group), :, q, :],
                out.at[pl.ds(l0, group), pl.ds(CELLS * q, CELLS), :],
                out_sem,
            ).start()
    pltpu.make_async_copy(out_v, out_v, out_sem).wait()


def body(*args):
    layers, cells_x, cells_y = args[0].shape
    nx, ny = lax.axis_size("gx"), lax.axis_size("gy")
    f32, i32 = jnp.float32, jnp.int32
    tile = pltpu.VMEM((layers, TILE, 128), f32)
    runs = pltpu.VMEM((layers, CELLS, RUNS, 128), f32)
    index = pltpu.VMEM((layers, CELLS, RUNS, 128), i32)
    layer = pltpu.VMEM((CELLS, RUNS, 128), f32)
    halo = pltpu.VMEM((2, layers, 128), f32)

    def rows(*shape):
        return pltpu.VMEM((*shape, 128), f32)

    hbm = pl.BlockSpec(memory_space=pltpu.HBM)
    smem = pl.BlockSpec(memory_space=pltpu.SMEM)
    shape = jax.ShapeDtypeStruct((layers, CELLS, RUNS, 128), f32)
    zi, zt = pl.pallas_call(
        runs_kernel,
        out_shape=(shape, shape),
        in_specs=[hbm, hbm, hbm, smem, smem, hbm, hbm, smem, hbm, smem],
        out_specs=(hbm, hbm),
        scratch_shapes=[
            runs,
            runs,
            index,
            index,
            pltpu.VMEM((CELLS, RUNS, 128), i32),
            index,
            runs,
            runs,
            runs,
            runs,
            tile,
            tile,
            tile,
            tile,
            runs,
            runs,
            runs,
            runs,
            runs,
            runs,
            runs,
            runs,
            runs,
            layer,
            layer,
            layer,
            layer,
            layer,
            halo,
            halo,
            halo,
            halo,
            *[rows(RUNS * layers)] * 5,
            rows(3 * layers),
            rows(nx, 3 * layers),
            rows(2 * layers),
            rows(nx, 2 * layers),
            rows(nx + 1, layers),
            rows(3 * layers // 2),
            rows(3 * layers // 2),
            rows(3 * layers // 2),
            rows(ny // 2, 3 * layers // 2),
            rows(layers),
            rows(layers),
            rows(layers),
            rows(ny // 2, layers),
            rows(ny // 2 + 1, layers // 2),
            rows(layers),
            rows(layers),
            rows(layers),
            rows(layers),
            pltpu.SemaphoreType.DMA((6,)),
            pltpu.SemaphoreType.DMA((2,)),
            pltpu.SemaphoreType.DMA((9,)),
            pltpu.SemaphoreType.DMA((9,)),
        ],
        compiler_params=pltpu.CompilerParams(
            collective_id=0, has_side_effects=True, vmem_limit_bytes=56 * 1024 * 1024
        ),
        cost_estimate=pl.CostEstimate(
            flops=100 * args[0].size, bytes_accessed=28 * args[0].size, transcendentals=0
        ),
        name="lines_xy",
    )(*args)
    return pl.pallas_call(
        layers_kernel,
        out_shape=jax.ShapeDtypeStruct(args[0].shape, f32),
        in_specs=[hbm, hbm],
        out_specs=hbm,
        scratch_shapes=[
            runs,
            runs,
            pltpu.VMEM((4, TILE, 128), f32),
            runs,
            layer,
            pltpu.SemaphoreType.DMA((8,)),
            pltpu.SemaphoreType.DMA,
        ],
        compiler_params=pltpu.CompilerParams(vmem_limit_bytes=62 * 1024 * 1024),
        cost_estimate=pl.CostEstimate(
            flops=2 * args[0].size, bytes_accessed=12 * args[0].size, transcendentals=0
        ),
        name="columns_z",
    )(zi, zt)


def solution(mesh):
    field = P(None, "gx", "gy")
    in_specs = (field, field, field, P(), P(), field, P("gx", "gy"), P(), field, P())
    return jax.shard_map(body, mesh=mesh, in_specs=in_specs, out_specs=field, check_vma=False)
```

time: 50.8 us -> 33.7 us (0.66)
  Pallas kernels: 48.3 us -> 33.6 us
  local copies, waits for them, and re-layouts: 2.3 us -> 0 us
    pallas_call x1 -> x2, Pallas kernels: 48.3 us -> 33.6 us  [the longest x1 30.9 us: body(): pl.pallas_call(runs_kernel, out_shape=(shape, shape), in_specs=[hbm, hbm,...]
    unnamed x1 -> x0, local copies, waits for them, and re-layouts: 2.3 us -> none
where the time goes in v1:
time: 33.7 us; the launch traced here: 33.6 us
  Pallas kernels  33.6 us (100%)
    pallas_call x1, Pallas kernels, body(): pl.pallas_call(runs_kernel, out_shape=(shape, shape), in_specs=[hbm, hbm,...  30.9 us
    pallas_call x1, Pallas kernels, body(): pl.pallas_call(layers_kernel, out_shape=jax.ShapeDtypeStruct(args[0].shap...  2.67 us

profile of v1, /device:TPU:1, one launch (start us, length us, event | category | flops | bytes accessed | tf_op | source)
XLA Modules:
  0.0 33.6 jit_solution(14064828420628352867)
XLA Ops:
  0.0 30.9 %lines_xy.1 = (f32[16,16,8,128]{3,2,1,0:T(8,128)}, f32[16,16,8,128]{3,2,1,0:T(8,128)}) custom-call(f32[16,128,128]{2,1,0:T(8,128)} %s_in.1, f32[16,128,128]{2,1,0:T(8,128)} %r_in.1, s32[16,128,128]{2,1,0:T(8,128)} %cls_in.1, f32[8]{0:T(128)} %k_tab.1, f32[15]{0:T(128)} %leak.1, s32[16,128,128]{2,1,0:T(8,128)} %well_in.1, s32[128,128]{1,0:T(8,128)} %rate_in.1, ...), custom_call_target="tpu_custom_call" | custom-call | flops 26214400 | bytes 7340032 | tf_op jit(solution)/shard_map/lines_xy/pallas_call | solution.py:669
  30.9 2.7 %columns_z.1 = f32[16,128,128]{2,1,0:T(8,128)} custom-call(f32[16,16,8,128]{3,2,1,0:T(8,128)} %get-tuple-element.7.zi_in, f32[16,16,8,128]{3,2,1,0:T(8,128)} %get-tuple-element.8.zt_in), custom_call_target="tpu_custom_call" | custom-call | flops 524288 | bytes 3145728 | tf_op jit(solution)/shard_map/columns_z/pallas_call | solution.py:739

commit v2 on v1

--- a/solution.py
+++ b/solution.py
@@ -98,8 +98,8 @@
     rate_tab,
     pit_in,
     level,
-    zi_out,
-    zt_out,
+    zi_v,
+    zt_v,
     s_v,
     w_v,
     cls_v,
@@ -121,8 +121,6 @@
     yi_v,
     yl_v,
     yr_v,
-    zt_v,
-    zi_v,
     pump_v,
     ez_v,
     flux_v,
@@ -156,7 +154,6 @@
     yl_end,
     yr_end,
     in_sem,
-    out_sem,
     send_sem,
     recv_sem,
 ):
@@ -254,14 +251,6 @@
     hi_send[0] = st_v[:, TILE - 1, :]
     hi_send[1] = rat_v[:, TILE - 1, :]
 
-    pl.semaphore_wait(barrier, nx + ny // 2)
-    halos = [
-        remote(lo_send, hi_recv, 0, {"gy": lax.rem(iy + ny - 1, ny)}),
-        remote(hi_send, lo_recv, 1, {"gy": lax.rem(iy + 1, ny)}),
-    ]
-    for halo in halos:
-        halo.start()
-
     loaded(2)
     loaded(3)
     own_x = jnp.where(ix == 0, 1.0, 0.0)
@@ -273,9 +262,6 @@
             w = jnp.where(pit, HELD, inverse(w_v[l]))
             ws.append(w)
             s_v[l] = w * jnp.where(pit, level[l], s_v[l])
-        wts = [turned(w) for w in ws]
-        for u, l in enumerate(ls):
-            wt_v[l] = wts[u]
         for u, l in enumerate(ls):
             ra, w = [ra_v[l, n] for n in range(CELLS)], [ws[u][n] for n in range(CELLS)]
             w_v[l] = ws[u]
@@ -341,9 +327,15 @@
         ref = dst.at[pl.ds(0, count)]
         pltpu.make_async_copy(ref, ref, recv_sem.at[n]).wait()
 
+    pl.semaphore_wait(barrier, nx + ny // 2)
+    halos = [
+        remote(lo_send, hi_recv, 0, {"gy": lax.rem(iy + ny - 1, ny)}),
+        remote(hi_send, lo_recv, 1, {"gy": lax.rem(iy + 1, ny)}),
+    ]
+    for halo in halos:
+        halo.start()
     gather_x(xm_send, xm_recv, 2)
 
-    ez_v[...] = jnp.zeros_like(ez_v)
     flux_v[...] = jnp.zeros_like(flux_v)
     own_y = jnp.where(iy == 0, 1.0, 0.0)
     for n in range(CELLS):
@@ -357,7 +349,6 @@
             above = jnp.minimum(l + 1, layers - 1)
             leak_l = jnp.where(l < layers - 1, leak[jnp.minimum(l, layers - 2)], 0.0)
             ra_up, s_up = strided(rat_v, above), strided(st_v, above)
-            wt = strided(wt_v, l)
             ra_before = down(ra[15])
             face = inverse(ra[0] + jnp.where(first, own_y * ra[0], ra_before))
             fy_v[l, 0] = face
@@ -379,20 +370,12 @@
                 ly_v[l, n] = ly
                 lz_v[l, n] = lz
                 q_v[l, pl.ds(n, RUNS, stride=CELLS), :] = ly + lz
-                wr_v[l, n] = wt[n]
-                e = wt[n] + ez_v[n]
-                inv = inverse(e + face_z)
-                t = face_z * inv
-                zt_v[l, n] = t
-                zi_v[l, n] = inv
-                ez_v[n] = e * t
+                zt_v[l, n] = face_z
             ra, s = ra_up, s_up
         for n in range(CELLS):
             ra_c[n], s_c[n] = ra[n], s[n]
 
     looped(layers, 2, across)
-    zt_copy = pltpu.make_async_copy(zt_v, zt_out, out_sem.at[0])
-    zt_copy.start()
 
     loaded(4)
     loaded(5)
@@ -440,14 +423,26 @@
         x_base.append(base)
     gather_x(xr_send, xr_recv, 3)
 
+    ez_v[...] = jnp.zeros_like(ez_v)
+
     def runs_y(ls):
+        wts = [turned(w_v[l]) for l in ls]
+        for u, l in enumerate(ls):
+            wt_v[l] = wts[u]
         for l in ls:
-            c, w, e, kept = reduce_matrix(
-                [fy_v[l, n] for n in range(CELLS)], [wr_v[l, n] for n in range(CELLS)]
-            )
+            wt = strided(wt_v, l)
+            c, w, e, kept = reduce_matrix([fy_v[l, n] for n in range(CELLS)], wt)
             for k in kept:
                 yi_v[l, k], yl_v[l, k], yr_v[l, k] = kept[k]
             node_w[at(l), :], node_c[at(l), :], node_e[at(l), :] = w, c, e
+            for n in range(CELLS):
+                wr_v[l, n] = wt[n]
+                e = wt[n] + ez_v[n]
+                inv = inverse(e + zt_v[l, n])
+                t = zt_v[l, n] * inv
+                zt_v[l, n] = t
+                zi_v[l, n] = inv
+                ez_v[n] = e * t
 
     looped(layers, 2, runs_y)
 
@@ -600,7 +595,6 @@
                 b = wr_v[l, n] * lines[u][n] - lz_v[l, n] + ez_v[n]
                 ez_v[n] = b * zt_v[l, n]
                 zi_v[l, n] = b * zi_v[l, n]
-            pltpu.make_async_copy(zi_v.at[l], zi_out.at[l], out_sem.at[1]).start()
 
     looped(layers, 2, fill_y)
 
@@ -611,29 +605,13 @@
     for ref, n, count in ((xm_recv, 2, nx), (xr_recv, 3, nx), (ym_recv, 5, chips), (yr_recv, 7, chips)):
         sent = ref.at[pl.ds(0, count - 1)]
         pltpu.make_async_copy(sent, sent, send_sem.at[n]).wait()
-    zt_copy.wait()
-    pltpu.make_async_copy(zi_v, zi_out, out_sem.at[1]).wait()
-
-
-def layers_kernel(zi_in, zt_in, out, zi_v, zt_v, tmp_v, out_v, ez_v, in_sem, out_sem):
-    layers = zi_in.shape[0]
+
+
+def layers_kernel(zi_v, zt_v, out, tmp_v, out_v, ez_v, out_sem):
+    layers = zi_v.shape[0]
     group = 4
-    parts = list(range(layers - group, -1, -group))
-    loads = []
-    for n, l in enumerate(parts):
-        part = pl.ds(l, group)
-        loads.append(
-            [
-                pltpu.make_async_copy(zi_in.at[part], zi_v.at[part], in_sem.at[2 * n]),
-                pltpu.make_async_copy(zt_in.at[part], zt_v.at[part], in_sem.at[2 * n + 1]),
-            ]
-        )
-        for load in loads[-1]:
-            load.start()
     ez_v[...] = jnp.zeros_like(ez_v)
-    for n, l0 in enumerate(parts):
-        for load in loads[n]:
-            load.wait()
+    for l0 in range(layers - group, -1, -group):
         for l in range(l0 + group - 1, l0 - 1, -1):
             for k in range(CELLS):
                 s = zi_v[l, k] + zt_v[l, k] * ez_v[k]
@@ -665,12 +643,13 @@
 
     hbm = pl.BlockSpec(memory_space=pltpu.HBM)
     smem = pl.BlockSpec(memory_space=pltpu.SMEM)
-    shape = jax.ShapeDtypeStruct((layers, CELLS, RUNS, 128), f32)
+    vmem = pl.BlockSpec(memory_space=pltpu.VMEM)
+    shape = pltpu.VMEM((layers, CELLS, RUNS, 128), f32)
     zi, zt = pl.pallas_call(
         runs_kernel,
         out_shape=(shape, shape),
         in_specs=[hbm, hbm, hbm, smem, smem, hbm, hbm, smem, hbm, smem],
-        out_specs=(hbm, hbm),
+        out_specs=(vmem, vmem),
         scratch_shapes=[
             runs,
             runs,
@@ -686,8 +665,6 @@
             tile,
             tile,
             tile,
-            runs,
-            runs,
             runs,
             runs,
             runs,
@@ -724,7 +701,6 @@
             rows(layers),
             rows(layers),
             pltpu.SemaphoreType.DMA((6,)),
-            pltpu.SemaphoreType.DMA((2,)),
             pltpu.SemaphoreType.DMA((9,)),
             pltpu.SemaphoreType.DMA((9,)),
         ],
@@ -739,18 +715,15 @@
     return pl.pallas_call(
         layers_kernel,
         out_shape=jax.ShapeDtypeStruct(args[0].shape, f32),
-        in_specs=[hbm, hbm],
+        in_specs=[vmem, vmem],
         out_specs=hbm,
         scratch_shapes=[
-            runs,
-            runs,
             pltpu.VMEM((4, TILE, 128), f32),
             runs,
             layer,
-            pltpu.SemaphoreType.DMA((8,)),
             pltpu.SemaphoreType.DMA,
         ],
-        compiler_params=pltpu.CompilerParams(vmem_limit_bytes=62 * 1024 * 1024),
+        compiler_params=pltpu.CompilerParams(vmem_limit_bytes=32 * 1024 * 1024),
         cost_estimate=pl.CostEstimate(
             flops=2 * args[0].size, bytes_accessed=12 * args[0].size, transcendentals=0
         ),

time: 33.7 us -> 31.3 us (0.929)
  Pallas kernels: 33.6 us -> 31.2 us
    pallas_call x1, Pallas kernels: 30.9 us -> 29.7 us  [body(): pl.pallas_call(runs_kernel, out_shape=(shape, shape), in_specs=[hbm, hbm,...]
    pallas_call x1, Pallas kernels: 2.67 us -> 1.56 us  [body(): pl.pallas_call(layers_kernel, out_shape=jax.ShapeDtypeStruct(args[0].shap...]
where the time goes in v2:
time: 31.3 us; the launch traced here: 31.2 us
  Pallas kernels  31.2 us (100%)
    pallas_call x1, Pallas kernels, body(): pl.pallas_call(runs_kernel, out_shape=(shape, shape), in_specs=[hbm, hbm,...  29.7 us
    pallas_call x1, Pallas kernels, body(): pl.pallas_call(layers_kernel, out_shape=jax.ShapeDtypeStruct(args[0].shap...  1.56 us

profile of v2, /device:TPU:1, one launch (start us, length us, event | category | flops | bytes accessed | tf_op | source)
XLA Modules:
  0.0 31.2 jit_solution(11261236889782797116)
XLA Ops:
  0.0 29.7 %lines_xy.1 = (f32[16,16,8,128]{3,2,1,0:T(8,128)S(1)}, f32[16,16,8,128]{3,2,1,0:T(8,128)S(1)}) custom-call(f32[16,128,128]{2,1,0:T(8,128)} %s_in.1, f32[16,128,128]{2,1,0:T(8,128)} %r_in.1, s32[16,128,128]{2,1,0:T(8,128)} %cls_in.1, f32[8]{0:T(128)} %k_tab.1, f32[15]{0:T(128)} %leak.1, s32[16,128,128]{2,1,0:T(8,128)} %well_in.1, s32[128,128]{1,0:T(8,128)} %rate_in.1, ...), custom_call_target="tpu_custom_call" | custom-call | flops 26214400 | bytes 7340032 | tf_op jit(solution)/shard_map/lines_xy/pallas_call | solution.py:648
  29.7 1.6 %columns_z.1 = f32[16,128,128]{2,1,0:T(8,128)} custom-call(f32[16,16,8,128]{3,2,1,0:T(8,128)S(1)} %get-tuple-element.7.zi_v, f32[16,16,8,128]{3,2,1,0:T(8,128)S(1)} %get-tuple-element.8.zt_v), custom_call_target="tpu_custom_call" | custom-call | flops 524288 | bytes 3145728 | tf_op jit(solution)/shard_map/columns_z/pallas_call | solution.py:715

commit v3 on v2

--- a/solution.py
+++ b/solution.py
@@ -10,6 +10,11 @@
 CELLS = 16
 RUNS = 8
 TILE = CELLS * RUNS
+SIDE = 4
+
+
+def far_first(steps, size):
+    return sorted(steps, key=lambda step: -sum(min(d, n - d) for d, n in zip(step, size)))
 
 
 def inverse(x):
@@ -79,9 +84,9 @@
     return pltpu.roll(x, RUNS - 1, 0)
 
 
-def looped(count, unroll, step):
+def looped(count, unroll, step, start=0):
     def body(i, _):
-        step([i * unroll + u for u in range(unroll)])
+        step([start + i * unroll + u for u in range(unroll)])
         return 0
 
     lax.fori_loop(0, count // unroll, body, 0)
@@ -149,10 +154,6 @@
     yr_send,
     yr_recv,
     ys_v,
-    pb_send,
-    pb_recv,
-    yl_end,
-    yr_end,
     in_sem,
     send_sem,
     recv_sem,
@@ -164,6 +165,22 @@
     mate = {"gy": iy + 1 - 2 * core}
     halves = range(layers // 8)
 
+    sides = (nx // SIDE, SIDE)
+    steps = [(p, q) for p in range(sides[0]) for q in range(sides[1])][1:]
+    along_x = [
+        lax.rem(ix // SIDE + p, sides[0]) * SIDE + lax.rem(lax.rem(ix, SIDE) + q, SIDE)
+        for p, q in far_first(steps, sides)
+    ]
+    chips = ny // 2
+    steps = [(p,) for p in range(1, chips)]
+    along_y = [lax.rem(iy + 2 * p, ny) for (p,) in far_first(steps, (chips,))]
+    before, after = lax.rem(iy + ny - 1, ny), lax.rem(iy + 1, ny)
+
+    barrier = pltpu.get_barrier_semaphore()
+    greeted = [{"gx": d} for d in along_x] + [{"gy": d} for d in along_y + [before, after]]
+    for where in greeted:
+        pl.semaphore_signal(barrier, inc=1, device_id=where, device_id_type=MESH)
+
     fields = [(cls_in, cls_v), (s_in, s_v), (r_in, w_v), (pit_in, pit_v), (well_in, well_v)]
     for n, (src, dst) in enumerate(fields):
         for q in range(RUNS):
@@ -178,24 +195,6 @@
     def loaded(n):
         ref = fields[n][1] if n < 5 else rate_v
         pltpu.make_async_copy(ref, ref, in_sem.at[n]).wait()
-
-    barrier = pltpu.get_barrier_semaphore()
-
-    def greet(where):
-        pl.semaphore_signal(barrier, inc=1, device_id=where, device_id_type=MESH)
-
-    def greet_x(k, _):
-        greet({"gx": lax.rem(ix + k, nx)})
-        return 0
-
-    def greet_y(k, _):
-        greet({"gy": lax.rem(iy + 2 * k, ny)})
-        return 0
-
-    lax.fori_loop(1, nx, greet_x, 0)
-    lax.fori_loop(1, ny // 2, greet_y, 0)
-    greet({"gy": lax.rem(iy + 1, ny)})
-    greet({"gy": lax.rem(iy + ny - 1, ny)})
 
     def remote(src, dst, n, where):
         return pltpu.make_async_remote_copy(
@@ -272,7 +271,7 @@
                 xi_v[l, k], xl_v[l, k], xr_v[l, k] = kept[k]
             node_w[at(l), :], node_c[at(l), :], node_e[at(l), :] = w, c, e
 
-    looped(layers, 2, weigh)
+    looped(layers, 4, weigh)
 
     def nodes(ref, h):
         return [ref[pl.ds(n + 64 * h, 8, stride=RUNS), :] for n in range(RUNS)]
@@ -306,31 +305,23 @@
         x_kept.append(kept)
 
     def gather_x(src, dst, n):
-        def send(k, _):
-            other = lax.rem(ix + k, nx)
+        for other in along_x:
             remote(src, dst.at[ix], n, {"gx": other}).start()
-            return 0
-
-        lax.fori_loop(1, nx, send, 0)
         dst[ix] = src[...]
 
     def gather_y(src, dst, n):
-        def send(k, _):
-            other = lax.rem(iy + 2 * k, ny)
+        for other in along_y:
             remote(src, dst.at[chip], n, {"gy": other}).start()
-            return 0
-
-        lax.fori_loop(1, ny // 2, send, 0)
         dst[chip] = src[...]
 
     def arrived(dst, n, count):
         ref = dst.at[pl.ds(0, count)]
         pltpu.make_async_copy(ref, ref, recv_sem.at[n]).wait()
 
-    pl.semaphore_wait(barrier, nx + ny // 2)
+    pl.semaphore_wait(barrier, len(greeted))
     halos = [
-        remote(lo_send, hi_recv, 0, {"gy": lax.rem(iy + ny - 1, ny)}),
-        remote(hi_send, lo_recv, 1, {"gy": lax.rem(iy + 1, ny)}),
+        remote(lo_send, hi_recv, 0, {"gy": before}),
+        remote(hi_send, lo_recv, 1, {"gy": after}),
     ]
     for halo in halos:
         halo.start()
@@ -375,7 +366,7 @@
         for n in range(CELLS):
             ra_c[n], s_c[n] = ra[n], s[n]
 
-    looped(layers, 2, across)
+    looped(layers, 4, across)
 
     loaded(4)
     loaded(5)
@@ -413,15 +404,14 @@
                 xi_v[l, k] = base[k]
             node_b[at(l), :], node_g[at(l), :] = b, g
 
-    looped(layers, 4, runs_x)
-
     x_base = []
     for h in halves:
+        looped(8, 4, runs_x, 8 * h)
         values, base = segment_rhs(h, x_kept[h])
         for n, x in enumerate(values):
-            xr_send[pl.ds(layers * n + 8 * h, 8), :] = x
+            xr_send[h, pl.ds(8 * n, 8), :] = x
         x_base.append(base)
-    gather_x(xr_send, xr_recv, 3)
+        gather_x(xr_send.at[h], xr_recv.at[h], 3 + h)
 
     ez_v[...] = jnp.zeros_like(ez_v)
 
@@ -444,7 +434,7 @@
                 zi_v[l, n] = inv
                 ez_v[n] = e * t
 
-    looped(layers, 2, runs_y)
+    looped(layers, 4, runs_y)
 
     is_a = core == 0
 
@@ -460,20 +450,25 @@
         values, kept = segment(h, inverse(end_y * hi_send[1, pl.ds(8 * h, 8), :]))
         y_values.append(values)
         y_kept.append(kept)
-    for n, pair in enumerate(zip(*y_values)):
-        pm_send[pl.ds(8 * n, 8), :] = theirs(pair)
-    pm_copy = remote(pm_send, pm_recv, 4, mate)
+    for h in halves:
+        for n, x in enumerate(y_values[h]):
+            pm_send[pl.ds(layers * n + 8 * h, 8), :] = x
+    pm_copy = remote(pm_send, pm_recv, 5, mate)
     pm_copy.start()
-    own = [mine(pair) for pair in zip(*y_values)]
     pm_copy.wait_recv()
-    other = [pm_recv[pl.ds(8 * n, 8), :] for n in range(3)]
-    c_a, c_b = mine((own[0], other[0])), theirs((own[0], other[0]))
-    el_a, el_b = mine((own[1], other[1])), theirs((own[1], other[1]))
-    er_a, er_b = mine((own[2], other[2])), theirs((own[2], other[2]))
-    c, w_left, w_right, mid = take_out(c_a, c_b, er_a + el_b)
-    for n, x in enumerate((c, el_a + w_left, er_b + w_right)):
-        ym_send[pl.ds(8 * n, 8), :] = x
-    gather_y(ym_send, ym_recv, 5)
+
+    def sides_of(own, other):
+        return mine((own, other)), theirs((own, other))
+
+    mids = []
+    for h in halves:
+        other = [pm_recv[pl.ds(layers * n + 8 * h, 8), :] for n in range(3)]
+        c, e, w = [sides_of(x, y) for x, y in zip(y_values[h], other)]
+        joined, w_left, w_right, mid = take_out(c[0], c[1], w[0] + e[1])
+        for n, x in enumerate((joined, e[0] + w_left, w[1] + w_right)):
+            ym_send[pl.ds(layers * n + 8 * h, 8), :] = x
+        mids.append(mid)
+    gather_y(ym_send, ym_recv, 6)
 
     arrived(xm_recv, 2, nx - 1)
     zero = jnp.zeros((RUNS, 128), jnp.float32)
@@ -486,17 +481,6 @@
         c = [rows(xm_recv, d, 0, h) for d in range(nx)]
         w = [rows(xm_recv, d, 2, h) + rows(xm_recv, d + 1, 1, h) for d in range(nx - 1)]
         x_chain.append(reduce_matrix(c, w + [zero])[3])
-
-    arrived(xr_recv, 3, nx - 1)
-    for h in halves:
-        kept = x_chain[h]
-        b = [rows(xr_recv, d, 1, h) + rows(xr_recv, d + 1, 0, h) for d in range(nx - 1)]
-        base = reduce_rhs(b + [zero], lambda k: kept[k])[2]
-        s = expand(
-            nx, lambda k: base[k], lambda k: kept[k][1], lambda k: kept[k][2], zero, zero
-        )
-        for d in range(-1, nx):
-            xs_v[d + 1, pl.ds(8 * h, 8), :] = s[d]
 
     def ends(s_left, s_right, h, base, kept):
         inv, tl, tr = kept[RUNS - 1]
@@ -507,10 +491,6 @@
         for n in range(RUNS):
             put(node_w, n, h, s[n])
             put(node_c, n, h, s[n - 1])
-
-    for h in halves:
-        part = pl.ds(8 * h, 8)
-        ends(xs_v[ix, part, :], xs_v[ix + 1, part, :], h, x_base[h], x_kept[h])
 
     def fill(l, base, tl, tr):
         s = expand(
@@ -535,56 +515,62 @@
                 yi_v[l, k] = base[k]
             node_b[at(l), :], node_g[at(l), :] = b, g
 
-    looped(layers, 4, fill_x)
-
-    y_base, y_values = [], []
-    for h in halves:
+    y_base, y_own, pr_copies = [], [], []
+    for h in halves:
+        arrived(xr_recv.at[h], 3 + h, nx - 1)
+        got = xr_recv.at[h]
+        kept = x_chain[h]
+        b = [got[d, pl.ds(8, 8), :] + got[d + 1, pl.ds(0, 8), :] for d in range(nx - 1)]
+        base = reduce_rhs(b + [zero], lambda k: kept[k])[2]
+        s = expand(
+            nx, lambda k: base[k], lambda k: kept[k][1], lambda k: kept[k][2], zero, zero
+        )
+        for d in range(-1, nx):
+            xs_v[d + 1, pl.ds(8 * h, 8), :] = s[d]
+        part = pl.ds(8 * h, 8)
+        ends(xs_v[ix, part, :], xs_v[ix + 1, part, :], h, x_base[h], x_kept[h])
+        looped(8, 4, fill_x, 8 * h)
         values, base = segment_rhs(h, y_kept[h])
-        y_values.append(values)
+        for n, x in enumerate(values):
+            pr_send[h, pl.ds(8 * n, 8), :] = x
+        y_own.append(values)
         y_base.append(base)
-    for n, pair in enumerate(zip(*y_values)):
-        pr_send[pl.ds(8 * n, 8), :] = theirs(pair)
-    pr_copy = remote(pr_send, pr_recv, 6, mate)
-    pr_copy.start()
-    own = [mine(pair) for pair in zip(*y_values)]
-
-    arrived(ym_recv, 5, ny // 2 - 1)
-    chips = ny // 2
-    c = [ym_recv[d, pl.ds(0, 8), :] for d in range(chips)]
-    w = [ym_recv[d, pl.ds(16, 8), :] + ym_recv[d + 1, pl.ds(8, 8), :] for d in range(chips - 1)]
-    y_chain = reduce_matrix(c, w + [zero])[3]
-
-    pr_copy.wait_recv()
-    other = [pr_recv[pl.ds(8 * n, 8), :] for n in range(2)]
-    gl_a, gl_b = mine((own[0], other[0])), theirs((own[0], other[0]))
-    gr_a, gr_b = mine((own[1], other[1])), theirs((own[1], other[1]))
-    b_mid = gr_a + gl_b
-    inv_mid, tl_mid, tr_mid = mid
-    yr_send[pl.ds(0, 8), :] = gl_a + b_mid * tl_mid
-    yr_send[pl.ds(8, 8), :] = gr_b + b_mid * tr_mid
-    gather_y(yr_send, yr_recv, 7)
-    arrived(yr_recv, 7, chips - 1)
-    b = [yr_recv[d, pl.ds(8, 8), :] + yr_recv[d + 1, pl.ds(0, 8), :] for d in range(chips - 1)]
-    base = reduce_rhs(b + [zero], lambda k: y_chain[k])[2]
-    s = expand(
-        chips, lambda k: base[k], lambda k: y_chain[k][1], lambda k: y_chain[k][2], zero, zero
-    )
-    for d in range(-1, chips):
-        ys_v[d + 1] = s[d]
-    s_left, s_right = ys_v[chip], ys_v[chip + 1]
-    s_mid = b_mid * inv_mid + tl_mid * s_left + tr_mid * s_right
-    pb_send[pl.ds(0, 8), :] = theirs((s_left, s_mid))
-    pb_send[pl.ds(8, 8), :] = theirs((s_mid, s_right))
-    pb_copy = remote(pb_send, pb_recv, 8, mate)
-    pb_copy.start()
-    yl_end[at(core), :] = mine((s_left, s_mid))
-    yr_end[at(core), :] = mine((s_mid, s_right))
-    pb_copy.wait_recv()
-    yl_end[at(1 - core), :] = pb_recv[pl.ds(0, 8), :]
-    yr_end[at(1 - core), :] = pb_recv[pl.ds(8, 8), :]
-    for h in halves:
-        part = pl.ds(8 * h, 8)
-        ends(yl_end[part, :], yr_end[part, :], h, y_base[h], y_kept[h])
+        pr_copies.append(remote(pr_send.at[h], pr_recv.at[h], 7 + h, mate))
+        pr_copies[h].start()
+
+    b_mids = []
+    for h in halves:
+        pr_copies[h].wait_recv()
+        other = [pr_recv[h, pl.ds(8 * n, 8), :] for n in range(2)]
+        (gl_a, gl_b), (gr_a, gr_b) = [sides_of(x, y) for x, y in zip(y_own[h], other)]
+        b_mid = gr_a + gl_b
+        inv, tl, tr = mids[h]
+        yr_send[h, pl.ds(0, 8), :] = gl_a + b_mid * tl
+        yr_send[h, pl.ds(8, 8), :] = gr_b + b_mid * tr
+        b_mids.append(b_mid)
+        gather_y(yr_send.at[h], yr_recv.at[h], 9 + h)
+    arrived(ym_recv, 6, chips - 1)
+    y_chain = []
+    for h in halves:
+        c = [rows(ym_recv, d, 0, h) for d in range(chips)]
+        w = [rows(ym_recv, d, 2, h) + rows(ym_recv, d + 1, 1, h) for d in range(chips - 1)]
+        y_chain.append(reduce_matrix(c, w + [zero])[3])
+
+    def chip_faces(h):
+        arrived(yr_recv.at[h], 9 + h, chips - 1)
+        got = yr_recv.at[h]
+        kept = y_chain[h]
+        b = [got[d, pl.ds(8, 8), :] + got[d + 1, pl.ds(0, 8), :] for d in range(chips - 1)]
+        base = reduce_rhs(b + [zero], lambda k: kept[k])[2]
+        s = expand(
+            chips, lambda k: base[k], lambda k: kept[k][1], lambda k: kept[k][2], zero, zero
+        )
+        for d in range(-1, chips):
+            ys_v[d + 1, pl.ds(8 * h, 8), :] = s[d]
+        s_left, s_right = ys_v[chip, pl.ds(8 * h, 8), :], ys_v[chip + 1, pl.ds(8 * h, 8), :]
+        inv, tl, tr = mids[h]
+        s_mid = b_mids[h] * inv + tl * s_left + tr * s_right
+        ends(mine((s_left, s_mid)), mine((s_mid, s_right)), h, y_base[h], y_kept[h])
 
     ez_v[...] = jnp.zeros_like(ez_v)
 
@@ -596,15 +582,20 @@
                 ez_v[n] = b * zt_v[l, n]
                 zi_v[l, n] = b * zi_v[l, n]
 
-    looped(layers, 2, fill_y)
+    for h in halves:
+        chip_faces(h)
+        looped(8, 2, fill_y, 8 * h)
 
     for halo in halos:
         halo.wait_send()
-    for copy in (pm_copy, pr_copy, pb_copy):
+    for copy in [pm_copy] + pr_copies:
         copy.wait_send()
-    for ref, n, count in ((xm_recv, 2, nx), (xr_recv, 3, nx), (ym_recv, 5, chips), (yr_recv, 7, chips)):
-        sent = ref.at[pl.ds(0, count - 1)]
-        pltpu.make_async_copy(sent, sent, send_sem.at[n]).wait()
+    sent = [(xm_recv, 2, nx), (ym_recv, 6, chips)]
+    for h in halves:
+        sent += [(xr_recv.at[h], 3 + h, nx), (yr_recv.at[h], 9 + h, chips)]
+    for ref, n, count in sent:
+        part = ref.at[pl.ds(0, count - 1)]
+        pltpu.make_async_copy(part, part, send_sem.at[n]).wait()
 
 
 def layers_kernel(zi_v, zt_v, out, tmp_v, out_v, ez_v, out_sem):
@@ -684,25 +675,21 @@
             *[rows(RUNS * layers)] * 5,
             rows(3 * layers),
             rows(nx, 3 * layers),
-            rows(2 * layers),
-            rows(nx, 2 * layers),
+            rows(2, layers),
+            rows(2, nx, layers),
             rows(nx + 1, layers),
-            rows(3 * layers // 2),
-            rows(3 * layers // 2),
-            rows(3 * layers // 2),
-            rows(ny // 2, 3 * layers // 2),
-            rows(layers),
-            rows(layers),
-            rows(layers),
-            rows(ny // 2, layers),
-            rows(ny // 2 + 1, layers // 2),
-            rows(layers),
-            rows(layers),
-            rows(layers),
-            rows(layers),
+            rows(3 * layers),
+            rows(3 * layers),
+            rows(3 * layers),
+            rows(ny // 2, 3 * layers),
+            rows(2, layers),
+            rows(2, layers),
+            rows(2, layers),
+            rows(2, ny // 2, layers),
+            rows(ny // 2 + 1, layers),
             pltpu.SemaphoreType.DMA((6,)),
-            pltpu.SemaphoreType.DMA((9,)),
-            pltpu.SemaphoreType.DMA((9,)),
+            pltpu.SemaphoreType.DMA((11,)),
+            pltpu.SemaphoreType.DMA((11,)),
         ],
         compiler_params=pltpu.CompilerParams(
             collective_id=0, has_side_effects=True, vmem_limit_bytes=56 * 1024 * 1024

time: 31.3 us -> 30.5 us (0.974)
  Pallas kernels: 31.2 us -> 30.4 us
    pallas_call x1, Pallas kernels: 29.7 us -> 28.8 us  [body(): pl.pallas_call(runs_kernel, out_shape=(shape, shape), in_specs=[hbm, hbm,...]
where the time goes in v3:
time: 30.5 us; the launch traced here: 30.4 us
  Pallas kernels  30.4 us (100%)
    pallas_call x1, Pallas kernels, body(): pl.pallas_call(runs_kernel, out_shape=(shape, shape), in_specs=[hbm, hbm,...  28.8 us
    pallas_call x1, Pallas kernels, body(): pl.pallas_call(layers_kernel, out_shape=jax.ShapeDtypeStruct(args[0].shap...  1.56 us

profile of v3, /device:TPU:1, one launch (start us, length us, event | category | flops | bytes accessed | tf_op | source)
XLA Modules:
  0.0 30.4 jit_solution(1329019007840926589)
XLA Ops:
  0.0 28.8 %lines_xy.1 = (f32[16,16,8,128]{3,2,1,0:T(8,128)S(1)}, f32[16,16,8,128]{3,2,1,0:T(8,128)S(1)}) custom-call(f32[16,128,128]{2,1,0:T(8,128)} %s_in.1, f32[16,128,128]{2,1,0:T(8,128)} %r_in.1, s32[16,128,128]{2,1,0:T(8,128)} %cls_in.1, f32[8]{0:T(128)} %k_tab.1, f32[15]{0:T(128)} %leak.1, s32[16,128,128]{2,1,0:T(8,128)} %well_in.1, s32[128,128]{1,0:T(8,128)} %rate_in.1, ...), custom_call_target="tpu_custom_call" | custom-call | flops 26214400 | bytes 7340032 | tf_op jit(solution)/shard_map/lines_xy/pallas_call | solution.py:639
  28.8 1.6 %columns_z.1 = f32[16,128,128]{2,1,0:T(8,128)} custom-call(f32[16,16,8,128]{3,2,1,0:T(8,128)S(1)} %get-tuple-element.7.zi_v, f32[16,16,8,128]{3,2,1,0:T(8,128)S(1)} %get-tuple-element.8.zt_v), custom_call_target="tpu_custom_call" | custom-call | flops 524288 | bytes 3145728 | tf_op jit(solution)/shard_map/columns_z/pallas_call | solution.py:702

commit v4 on v3

--- a/solution.py
+++ b/solution.py
@@ -515,7 +515,19 @@
                 yi_v[l, k] = base[k]
             node_b[at(l), :], node_g[at(l), :] = b, g
 
-    y_base, y_own, pr_copies = [], [], []
+    y_base, y_own, pr_copies, b_mids = [], [], [], []
+
+    def join_pair(h):
+        pr_copies[h].wait_recv()
+        other = [pr_recv[h, pl.ds(8 * n, 8), :] for n in range(2)]
+        (gl_a, gl_b), (gr_a, gr_b) = [sides_of(x, y) for x, y in zip(y_own[h], other)]
+        b_mid = gr_a + gl_b
+        inv, tl, tr = mids[h]
+        yr_send[h, pl.ds(0, 8), :] = gl_a + b_mid * tl
+        yr_send[h, pl.ds(8, 8), :] = gr_b + b_mid * tr
+        b_mids.append(b_mid)
+        gather_y(yr_send.at[h], yr_recv.at[h], 9 + h)
+
     for h in halves:
         arrived(xr_recv.at[h], 3 + h, nx - 1)
         got = xr_recv.at[h]
@@ -529,7 +541,10 @@
             xs_v[d + 1, pl.ds(8 * h, 8), :] = s[d]
         part = pl.ds(8 * h, 8)
         ends(xs_v[ix, part, :], xs_v[ix + 1, part, :], h, x_base[h], x_kept[h])
-        looped(8, 4, fill_x, 8 * h)
+        looped(4, 4, fill_x, 8 * h)
+        if h:
+            join_pair(0)
+        looped(4, 4, fill_x, 8 * h + 4)
         values, base = segment_rhs(h, y_kept[h])
         for n, x in enumerate(values):
             pr_send[h, pl.ds(8 * n, 8), :] = x
@@ -538,17 +553,8 @@
         pr_copies.append(remote(pr_send.at[h], pr_recv.at[h], 7 + h, mate))
         pr_copies[h].start()
 
-    b_mids = []
-    for h in halves:
-        pr_copies[h].wait_recv()
-        other = [pr_recv[h, pl.ds(8 * n, 8), :] for n in range(2)]
-        (gl_a, gl_b), (gr_a, gr_b) = [sides_of(x, y) for x, y in zip(y_own[h], other)]
-        b_mid = gr_a + gl_b
-        inv, tl, tr = mids[h]
-        yr_send[h, pl.ds(0, 8), :] = gl_a + b_mid * tl
-        yr_send[h, pl.ds(8, 8), :] = gr_b + b_mid * tr
-        b_mids.append(b_mid)
-        gather_y(yr_send.at[h], yr_recv.at[h], 9 + h)
+    join_pair(1)
+
     arrived(ym_recv, 6, chips - 1)
     y_chain = []
     for h in halves:

time: 30.5 us -> 30.2 us (level)
    pallas_call x1, Pallas kernels: 28.8 us -> 28.5 us  [body(): pl.pallas_call(runs_kernel, out_shape=(shape, shape), in_specs=[hbm, hbm,...]
where the time goes in v4:
time: 30.2 us; the launch traced here: 30.1 us
  Pallas kernels  30.1 us (100%)
    pallas_call x1, Pallas kernels, body(): pl.pallas_call(runs_kernel, out_shape=(shape, shape), in_specs=[hbm, hbm,...  28.5 us
    pallas_call x1, Pallas kernels, body(): pl.pallas_call(layers_kernel, out_shape=jax.ShapeDtypeStruct(args[0].shap...  1.56 us

profile of v4, /device:TPU:1, one launch (start us, length us, event | category | flops | bytes accessed | tf_op | source)
XLA Modules:
  0.0 30.1 jit_solution(12420354628537610642)
XLA Ops:
  0.0 28.5 %lines_xy.1 = (f32[16,16,8,128]{3,2,1,0:T(8,128)S(1)}, f32[16,16,8,128]{3,2,1,0:T(8,128)S(1)}) custom-call(f32[16,128,128]{2,1,0:T(8,128)} %s_in.1, f32[16,128,128]{2,1,0:T(8,128)} %r_in.1, s32[16,128,128]{2,1,0:T(8,128)} %cls_in.1, f32[8]{0:T(128)} %k_tab.1, f32[15]{0:T(128)} %leak.1, s32[16,128,128]{2,1,0:T(8,128)} %well_in.1, s32[128,128]{1,0:T(8,128)} %rate_in.1, ...), custom_call_target="tpu_custom_call" | custom-call | flops 26214400 | bytes 7340032 | tf_op jit(solution)/shard_map/lines_xy/pallas_call | solution.py:645
  28.5 1.6 %columns_z.1 = f32[16,128,128]{2,1,0:T(8,128)} custom-call(f32[16,16,8,128]{3,2,1,0:T(8,128)S(1)} %get-tuple-element.7.zi_v, f32[16,16,8,128]{3,2,1,0:T(8,128)S(1)} %get-tuple-element.8.zt_v), custom_call_target="tpu_custom_call" | custom-call | flops 524288 | bytes 3145728 | tf_op jit(solution)/shard_map/columns_z/pallas_call | solution.py:708

commit v5 on v4

--- a/solution.py
+++ b/solution.py
@@ -606,7 +606,7 @@
 
 def layers_kernel(zi_v, zt_v, out, tmp_v, out_v, ez_v, out_sem):
     layers = zi_v.shape[0]
-    group = 4
+    group = 8
     ez_v[...] = jnp.zeros_like(ez_v)
     for l0 in range(layers - group, -1, -group):
         for l in range(l0 + group - 1, l0 - 1, -1):
@@ -711,7 +711,7 @@
         in_specs=[vmem, vmem],
         out_specs=hbm,
         scratch_shapes=[
-            pltpu.VMEM((4, TILE, 128), f32),
+            pltpu.VMEM((8, TILE, 128), f32),
             runs,
             layer,
             pltpu.SemaphoreType.DMA,

time: 30.2 us -> 30 us (level)
  no operation moved by 1% of the time
where the time goes in v5:
time: 30 us
  Pallas kernels  30 us (100%)
    pallas_call x1, Pallas kernels, body(): pl.pallas_call(runs_kernel, out_shape=(shape, shape), in_specs=[hbm, hbm,...  28.5 us
    pallas_call x1, Pallas kernels, body(): pl.pallas_call(layers_kernel, out_shape=jax.ShapeDtypeStruct(args[0].shap...  1.44 us

profile of v5, /device:TPU:1, one launch (start us, length us, event | category | flops | bytes accessed | tf_op | source)
XLA Modules:
  0.0 30.0 jit_solution(17801140328844998990)
XLA Ops:
  0.0 28.5 %lines_xy.1 = (f32[16,16,8,128]{3,2,1,0:T(8,128)S(1)}, f32[16,16,8,128]{3,2,1,0:T(8,128)S(1)}) custom-call(f32[16,128,128]{2,1,0:T(8,128)} %s_in.1, f32[16,128,128]{2,1,0:T(8,128)} %r_in.1, s32[16,128,128]{2,1,0:T(8,128)} %cls_in.1, f32[8]{0:T(128)} %k_tab.1, f32[15]{0:T(128)} %leak.1, s32[16,128,128]{2,1,0:T(8,128)} %well_in.1, s32[128,128]{1,0:T(8,128)} %rate_in.1, ...), custom_call_target="tpu_custom_call" | custom-call | flops 26214400 | bytes 7340032 | tf_op jit(solution)/shard_map/lines_xy/pallas_call | solution.py:645
  28.5 1.4 %columns_z.1 = f32[16,128,128]{2,1,0:T(8,128)} custom-call(f32[16,16,8,128]{3,2,1,0:T(8,128)S(1)} %get-tuple-element.7.zi_v, f32[16,16,8,128]{3,2,1,0:T(8,128)S(1)} %get-tuple-element.8.zt_v), custom_call_target="tpu_custom_call" | custom-call | flops 524288 | bytes 3145728 | tf_op jit(solution)/shard_map/columns_z/pallas_call | solution.py:708

commit v6 on v5

--- a/solution.py
+++ b/solution.py
@@ -296,28 +296,6 @@
         base[RUNS - 1] = b * inv
         return (extra[0] + g + b * tl, b * tr), base
 
-    x_kept = []
-    end_x = jnp.where(ix == nx - 1, 2.0, 1.0)
-    for h in halves:
-        values, kept = segment(h, inverse(end_x * ra_v[pl.ds(8 * h, 8), CELLS - 1, RUNS - 1, :]))
-        for n, x in enumerate(values):
-            xm_send[pl.ds(layers * n + 8 * h, 8), :] = x
-        x_kept.append(kept)
-
-    def gather_x(src, dst, n):
-        for other in along_x:
-            remote(src, dst.at[ix], n, {"gx": other}).start()
-        dst[ix] = src[...]
-
-    def gather_y(src, dst, n):
-        for other in along_y:
-            remote(src, dst.at[chip], n, {"gy": other}).start()
-        dst[chip] = src[...]
-
-    def arrived(dst, n, count):
-        ref = dst.at[pl.ds(0, count)]
-        pltpu.make_async_copy(ref, ref, recv_sem.at[n]).wait()
-
     pl.semaphore_wait(barrier, len(greeted))
     halos = [
         remote(lo_send, hi_recv, 0, {"gy": before}),
@@ -325,6 +303,29 @@
     ]
     for halo in halos:
         halo.start()
+
+    x_kept = []
+    end_x = jnp.where(ix == nx - 1, 2.0, 1.0)
+    for h in halves:
+        values, kept = segment(h, inverse(end_x * ra_v[pl.ds(8 * h, 8), CELLS - 1, RUNS - 1, :]))
+        for n, x in enumerate(values):
+            xm_send[pl.ds(layers * n + 8 * h, 8), :] = x
+        x_kept.append(kept)
+
+    def gather_x(src, dst, n):
+        for other in along_x:
+            remote(src, dst.at[ix], n, {"gx": other}).start()
+        dst[ix] = src[...]
+
+    def gather_y(src, dst, n):
+        for other in along_y:
+            remote(src, dst.at[chip], n, {"gy": other}).start()
+        dst[chip] = src[...]
+
+    def arrived(dst, n, count):
+        ref = dst.at[pl.ds(0, count)]
+        pltpu.make_async_copy(ref, ref, recv_sem.at[n]).wait()
+
     gather_x(xm_send, xm_recv, 2)
 
     flux_v[...] = jnp.zeros_like(flux_v)

time: 30 us -> 30.1 us (level)
  no operation moved by 1% of the time
where the time goes in v6:
time: 30.1 us; the launch traced here: 30 us
  Pallas kernels  30 us (100%)
    pallas_call x1, Pallas kernels, body(): pl.pallas_call(runs_kernel, out_shape=(shape, shape), in_specs=[hbm, hbm,...  28.6 us
    pallas_call x1, Pallas kernels, body(): pl.pallas_call(layers_kernel, out_shape=jax.ShapeDtypeStruct(args[0].shap...  1.44 us

profile of v6, /device:TPU:1, one launch (start us, length us, event | category | flops | bytes accessed | tf_op | source)
XLA Modules:
  0.0 30.0 jit_solution(3441509918280326594)
XLA Ops:
  0.0 28.6 %lines_xy.1 = (f32[16,16,8,128]{3,2,1,0:T(8,128)S(1)}, f32[16,16,8,128]{3,2,1,0:T(8,128)S(1)}) custom-call(f32[16,128,128]{2,1,0:T(8,128)} %s_in.1, f32[16,128,128]{2,1,0:T(8,128)} %r_in.1, s32[16,128,128]{2,1,0:T(8,128)} %cls_in.1, f32[8]{0:T(128)} %k_tab.1, f32[15]{0:T(128)} %leak.1, s32[16,128,128]{2,1,0:T(8,128)} %well_in.1, s32[128,128]{1,0:T(8,128)} %rate_in.1, ...), custom_call_target="tpu_custom_call" | custom-call | flops 26214400 | bytes 7340032 | tf_op jit(solution)/shard_map/lines_xy/pallas_call | solution.py:646
  28.6 1.4 %columns_z.1 = f32[16,128,128]{2,1,0:T(8,128)} custom-call(f32[16,16,8,128]{3,2,1,0:T(8,128)S(1)} %get-tuple-element.7.zi_v, f32[16,16,8,128]{3,2,1,0:T(8,128)S(1)} %get-tuple-element.8.zt_v), custom_call_target="tpu_custom_call" | custom-call | flops 524288 | bytes 3145728 | tf_op jit(solution)/shard_map/columns_z/pallas_call | solution.py:709

commit v7 on v4

--- a/solution.py
+++ b/solution.py
@@ -615,13 +615,11 @@
                 ez_v[k] = s
                 tmp_v[l - l0, pl.ds(k, RUNS, stride=CELLS), :] = s
         for l in range(l0 + group - 1, l0 - 1, -1):
-            out_v[l] = tmp_v[l - l0].T.reshape(CELLS, RUNS, 128)
-        for q in range(RUNS):
-            pltpu.make_async_copy(
-                out_v.at[pl.ds(l0, group), :, q, :],
-                out.at[pl.ds(l0, group), pl.ds(CELLS * q, CELLS), :],
-                out_sem,
-            ).start()
+            rows = tmp_v[l - l0].T.reshape(CELLS, RUNS, 128)
+            for n in range(CELLS):
+                out_v[l, pl.ds(n, RUNS, stride=CELLS), :] = rows[n]
+        part = pl.ds(l0, group)
+        pltpu.make_async_copy(out_v.at[part], out.at[part], out_sem).start()
     pltpu.make_async_copy(out_v, out_v, out_sem).wait()
 
 
@@ -712,7 +710,7 @@
         out_specs=hbm,
         scratch_shapes=[
             pltpu.VMEM((4, TILE, 128), f32),
-            runs,
+            tile,
             layer,
             pltpu.SemaphoreType.DMA,
         ],

time: 30.2 us -> 30 us (level)
  no operation moved by 1% of the time
where the time goes in v7:
time: 30 us; the launch traced here: 29.9 us
  Pallas kernels  29.9 us (100%)
    pallas_call x1, Pallas kernels, body(): pl.pallas_call(runs_kernel, out_shape=(shape, shape), in_specs=[hbm, hbm,...  28.5 us
    pallas_call x1, Pallas kernels, body(): pl.pallas_call(layers_kernel, out_shape=jax.ShapeDtypeStruct(args[0].shap...  1.36 us

profile of v7, /device:TPU:1, one launch (start us, length us, event | category | flops | bytes accessed | tf_op | source)
XLA Modules:
  0.0 29.9 jit_solution(248534179778672355)
XLA Ops:
  0.0 28.5 %lines_xy.1 = (f32[16,16,8,128]{3,2,1,0:T(8,128)S(1)}, f32[16,16,8,128]{3,2,1,0:T(8,128)S(1)}) custom-call(f32[16,128,128]{2,1,0:T(8,128)} %s_in.1, f32[16,128,128]{2,1,0:T(8,128)} %r_in.1, s32[16,128,128]{2,1,0:T(8,128)} %cls_in.1, f32[8]{0:T(128)} %k_tab.1, f32[15]{0:T(128)} %leak.1, s32[16,128,128]{2,1,0:T(8,128)} %well_in.1, s32[128,128]{1,0:T(8,128)} %rate_in.1, ...), custom_call_target="tpu_custom_call" | custom-call | flops 26214400 | bytes 7340032 | tf_op jit(solution)/shard_map/lines_xy/pallas_call | solution.py:643
  28.5 1.4 %columns_z.1 = f32[16,128,128]{2,1,0:T(8,128)} custom-call(f32[16,16,8,128]{3,2,1,0:T(8,128)S(1)} %get-tuple-element.7.zi_v, f32[16,16,8,128]{3,2,1,0:T(8,128)S(1)} %get-tuple-element.8.zt_v), custom_call_target="tpu_custom_call" | custom-call | flops 524288 | bytes 3145728 | tf_op jit(solution)/shard_map/columns_z/pallas_call | solution.py:706
